TPU v7x, 32 devices: a whole 2x2x4 slice. The times are simulated.
32 devices in a mesh: batch: 8 (over y, x, core), chan: 4 (over z).
Axes of the slice: x: 2, y: 2, z: 4, core: 2. Of those that a mesh axis runs over, the one named last changes fastest.
Arguments:
- tokens: bfloat16 [32768, 768], P(('batch', 'chan')), may hold values from -6 to 6
- w_in: bfloat16 [768, 768], P(None, 'chan'), may hold values from -0.21875 to 0.21875
- w_forget: bfloat16 [768, 384], P(None, 'chan'), may hold values from -0.21875 to 0.21875
- b_forget: float32 [384], P('chan'), may hold values from 2.5 to 10
- rotation: float32 [384], P('chan'), may hold values from -3.140625 to 3.140625
- w_outgate: bfloat16 [768, 768], P(None, 'chan'), may hold values from -0.21875 to 0.21875
- gn_gain: float32 [768], P('chan'), may hold values from 0.5 to 1.5
- w_out: bfloat16 [768, 768], P('chan'), may hold values from -0.21875 to 0.21875
- rms_gain: float32 [768], replicated, may hold values from 0.5 to 1.5
- w_gate: bfloat16 [768, 1536], P(None, 'chan'), may hold values from -0.21875 to 0.21875
- w_up: bfloat16 [768, 1536], P(None, 'chan'), may hold values from -0.21875 to 0.21875
- w_down: bfloat16 [1536, 768], P('chan'), may hold values from -0.15625 to 0.15625
- cotangent: bfloat16 [32768, 768], P(('batch', 'chan')), may hold values from -6 to 6
- buckets: int32 [8], P('batch'), may hold values from 1024 to 4096, as said below
- lengths: int32 [8, 4], P('batch'), may hold values from 0 to 4096, as said below
Outputs:
- block_out: bfloat16 [32768, 768], P(('batch', 'chan'))
- grad_tokens: float32 [32768, 768], P(('batch', 'chan'))
- grad_w_in: float32 [768, 768], P(None, 'chan')
- grad_w_forget: float32 [768, 384], P(None, 'chan')
- grad_b_forget: float32 [384], P('chan')
- grad_rotation: float32 [384], P('chan')
- grad_w_outgate: float32 [768, 768], P(None, 'chan')
- grad_gn_gain: float32 [768], P('chan')
- grad_w_out: float32 [768, 768], P('chan')
- grad_rms_gain: float32 [768], P('chan')
- grad_w_gate: float32 [768, 1536], P(None, 'chan')
- grad_w_up: float32 [768, 1536], P(None, 'chan')
- grad_w_down: float32 [1536, 768], P('chan')
Inputs may be any that keep to these rules, and one draw needn't show every extreme that they name: `buckets`: each group's bucket is 4096, 2048 or 1024, and the group holds 4096 // bucket sequences; the first group's bucket is 4096. `lengths`: slot j of a group is the true length of its sequence j; the group's first sequence fills its bucket, the others are longer than half the bucket and at most the bucket; slots past the group's sequences are 0.
All inputs are finite; a program needn't handle non-finite values.
Results may differ from a plain program's by a relative error of at most 0.015.
Values may be sent and summed in bfloat16 or wider, within the bound.
A program may use at most 256 MiB of HBM per device.

v0:
```python
import jax
import jax.numpy as jnp
from jax import lax
from jax.sharding import PartitionSpec as P

HEAD_CH = 32


def complex_combine(former, latter):
    return (
        latter[0] * former[0] - latter[1] * former[1],
        latter[0] * former[1] + latter[1] * former[0],
        latter[0] * former[2] - latter[1] * former[3] + latter[2],
        latter[0] * former[3] + latter[1] * former[2] + latter[3],
    )


def recurrence(rho_r, rho_i, push_r, push_i):
    row_count, width_ch = rho_r.shape
    block_len = 16
    block_count = row_count // block_len
    shaped = [
        piece.reshape(block_count, block_len, width_ch) for piece in (rho_r, rho_i, push_r, push_i)
    ]
    state_real = jnp.zeros((block_count, width_ch), jnp.float32)
    state_imag = jnp.zeros((block_count, width_ch), jnp.float32)
    prod_real = jnp.ones((block_count, width_ch), jnp.float32)
    prod_imag = jnp.zeros((block_count, width_ch), jnp.float32)
    local_real, local_imag, cum_real, cum_imag = ([], [], [], [])
    for position in range(block_len):
        rate_real = shaped[0][:, position]
        rate_imag = shaped[1][:, position]
        state_real, state_imag = (
            rate_real * state_real - rate_imag * state_imag + shaped[2][:, position],
            rate_real * state_imag + rate_imag * state_real + shaped[3][:, position],
        )
        prod_real, prod_imag = (
            rate_real * prod_real - rate_imag * prod_imag,
            rate_real * prod_imag + rate_imag * prod_real,
        )
        local_real.append(state_real)
        local_imag.append(state_imag)
        cum_real.append(prod_real)
        cum_imag.append(prod_imag)
    totals = lax.associative_scan(
        complex_combine, (prod_real, prod_imag, state_real, state_imag), axis=0
    )
    zero_row = jnp.zeros((1, width_ch), jnp.float32)
    carry_real = jnp.concatenate([zero_row, totals[2][:-1]], axis=0)[:, None, :]
    carry_imag = jnp.concatenate([zero_row, totals[3][:-1]], axis=0)[:, None, :]
    local_r = jnp.stack(local_real, axis=1)
    local_i = jnp.stack(local_imag, axis=1)
    cumul_r = jnp.stack(cum_real, axis=1)
    cumul_i = jnp.stack(cum_imag, axis=1)
    out_real = local_r + cumul_r * carry_real - cumul_i * carry_imag
    out_imag = local_i + cumul_r * carry_imag + cumul_i * carry_real
    return (out_real.reshape(row_count, width_ch), out_imag.reshape(row_count, width_ch))


def mixer_core(proj_in, proj_f, proj_g, b_forget, rotation, gn_gain, starts):
    row_count = proj_in.shape[0]
    head_count = proj_in.shape[1] // (2 * HEAD_CH)
    values_in = jax.nn.silu(proj_in).reshape(row_count, head_count, 2, HEAD_CH)
    real_in = values_in[:, :, 0, :].reshape(row_count, head_count * HEAD_CH)
    imag_in = values_in[:, :, 1, :].reshape(row_count, head_count * HEAD_CH)
    forget = jax.nn.sigmoid(proj_f + b_forget)
    keep_rate = forget * (1.0 - starts)[:, None]
    state_r, state_i = recurrence(
        keep_rate * jnp.cos(rotation),
        keep_rate * jnp.sin(rotation),
        (1.0 - forget) * real_in,
        (1.0 - forget) * imag_in,
    )
    stacked = jnp.stack(
        [
            state_r.reshape(row_count, head_count, HEAD_CH),
            state_i.reshape(row_count, head_count, HEAD_CH),
        ],
        axis=2,
    )
    stacked = stacked.reshape(row_count, head_count, 2 * HEAD_CH)
    gated = jax.nn.silu(proj_g).reshape(row_count, head_count, 2 * HEAD_CH) * stacked
    group_mean = jnp.mean(gated, axis=-1, keepdims=True)
    centred = gated - group_mean
    variance = jnp.mean(centred * centred, axis=-1, keepdims=True)
    normed = centred * lax.rsqrt(variance + 1e-05)
    return normed.reshape(row_count, head_count * 2 * HEAD_CH) * gn_gain


def row_flags(positions, bucket, seq_lengths):
    slot_index = positions // bucket
    offset = positions - slot_index * bucket
    slot_ids = jnp.arange(seq_lengths.shape[0], dtype=jnp.int32)
    onehot = slot_index[:, None] == slot_ids[None, :]
    live_limit = jnp.sum(jnp.where(onehot, seq_lengths[None, :], 0), axis=1)
    return ((offset == 0).astype(jnp.float32), (offset < live_limit).astype(jnp.float32))


def rms_piece(resid_rows, gain_vec):
    return (
        resid_rows
        * lax.rsqrt(jnp.mean(resid_rows * resid_rows, axis=-1, keepdims=True) + 1e-06)
        * gain_vec
    )


def swiglu(gate_act, up_act):
    return jax.nn.silu(gate_act) * up_act


def contract(left, right, left_dim, right_dim):
    return lax.dot_general(
        left, right, (((left_dim,), (right_dim,)), ((), ())), preferred_element_type=jnp.float32
    )


def local(
    tokens,
    w_in,
    w_forget,
    b_forget,
    rotation,
    w_outgate,
    gn_gain,
    w_out,
    rms_gain,
    w_gate,
    w_up,
    w_down,
    cotangent,
    buckets,
    lengths,
):
    chan_count = lax.axis_size("chan")
    chan_rank = lax.axis_index("chan")
    own_rows = tokens.shape[0]
    group_rows = own_rows * chan_count
    bucket = buckets[0]
    seq_lengths = lengths[0]
    starts = row_flags(jnp.arange(group_rows, dtype=jnp.int32), bucket, seq_lengths)[0]
    live_rows = row_flags(
        chan_rank * own_rows + jnp.arange(own_rows, dtype=jnp.int32), bucket, seq_lengths
    )[1]
    all_tokens = lax.all_gather(tokens, "chan", axis=0, tiled=True)
    mix_weights = jnp.concatenate([w_in, w_forget, w_outgate], axis=1)
    width_in = w_in.shape[1]
    width_f = w_forget.shape[1]
    projected = jnp.dot(all_tokens, mix_weights, preferred_element_type=jnp.float32)

    def core_fn(proj_all, bias_f, angle_f, gain_f):
        return mixer_core(
            proj_all[:, :width_in],
            proj_all[:, width_in : width_in + width_f],
            proj_all[:, width_in + width_f :],
            bias_f,
            angle_f,
            gain_f,
            starts,
        )

    mix_norm, core_back = jax.vjp(core_fn, projected, b_forget, rotation, gn_gain)
    mix_low = mix_norm.astype(jnp.bfloat16)
    mixed_rows = lax.psum_scatter(
        jnp.dot(mix_low, w_out, preferred_element_type=jnp.float32),
        "chan",
        scatter_dimension=0,
        tiled=True,
    )
    residual = tokens.astype(jnp.float32) + mixed_rows
    ffn_norm, rms_back = jax.vjp(rms_piece, residual, rms_gain)
    ffn_in = ffn_norm.astype(jnp.bfloat16)
    seed_rows = cotangent * live_rows.astype(jnp.bfloat16)[:, None]
    norm_all = lax.all_gather(ffn_in, "chan", axis=0, tiled=True)
    gate_act = jnp.dot(norm_all, w_gate, preferred_element_type=jnp.float32)
    up_act = jnp.dot(norm_all, w_up, preferred_element_type=jnp.float32)
    hidden_f, glu_back = jax.vjp(swiglu, gate_act, up_act)
    hidden = hidden_f.astype(jnp.bfloat16)
    block_out = (
        residual
        + lax.psum_scatter(
            jnp.dot(hidden, w_down, preferred_element_type=jnp.float32).astype(jnp.bfloat16),
            "chan",
            scatter_dimension=0,
            tiled=True,
        ).astype(jnp.float32)
    ).astype(jnp.bfloat16)
    seed_all = lax.all_gather(seed_rows, "chan", axis=0, tiled=True)
    d_hidden = contract(seed_all, w_down, 1, 1)
    d_gate_f, d_up_f = glu_back(d_hidden)
    d_gate = d_gate_f.astype(jnp.bfloat16)
    d_up = d_up_f.astype(jnp.bfloat16)
    grad_w_down = contract(hidden, seed_all, 0, 0)
    grad_w_gate = contract(norm_all, d_gate, 0, 0)
    grad_w_up = contract(norm_all, d_up, 0, 0)
    d_ffn_in = lax.psum_scatter(
        (contract(d_gate, w_gate, 1, 1) + contract(d_up, w_up, 1, 1)).astype(jnp.bfloat16),
        "chan",
        scatter_dimension=0,
        tiled=True,
    ).astype(jnp.float32)
    d_resid_norm, grad_rms_part = rms_back(d_ffn_in)
    d_resid = seed_rows.astype(jnp.float32) + d_resid_norm
    d_mixed_low = d_resid.astype(jnp.bfloat16)
    d_mixed_all = lax.all_gather(d_mixed_low, "chan", axis=0, tiled=True)
    grad_w_out = contract(mix_low, d_mixed_all, 0, 0)
    d_mix_norm = contract(d_mixed_all, w_out, 1, 1)
    d_projected, grad_b_forget, grad_rotation, grad_gn_gain = core_back(d_mix_norm)
    d_proj_low = d_projected.astype(jnp.bfloat16)
    grad_mix = contract(all_tokens, d_proj_low, 0, 0)
    grad_w_in = grad_mix[:, :width_in]
    grad_w_forget = grad_mix[:, width_in : width_in + width_f]
    grad_w_outgate = grad_mix[:, width_in + width_f :]
    d_tokens_part = contract(d_proj_low, mix_weights, 1, 1)
    d_tokens_own, grad_rms_gain = (
        lax.psum_scatter(
            d_tokens_part.astype(jnp.bfloat16), "chan", scatter_dimension=0, tiled=True
        ).astype(jnp.float32),
        lax.psum_scatter(
            grad_rms_part.astype(jnp.bfloat16), "chan", scatter_dimension=0, tiled=True
        ).astype(jnp.float32),
    )
    grad_tokens = d_resid + d_tokens_own
    (
        grad_w_in,
        grad_w_forget,
        grad_b_forget,
        grad_rotation,
        grad_w_outgate,
        grad_gn_gain,
        grad_w_out,
        grad_rms_gain,
        grad_w_gate,
        grad_w_up,
        grad_w_down,
    ) = lax.psum(
        (
            grad_w_in,
            grad_w_forget,
            grad_b_forget,
            grad_rotation,
            grad_w_outgate,
            grad_gn_gain,
            grad_w_out,
            grad_rms_gain,
            grad_w_gate,
            grad_w_up,
            grad_w_down,
        ),
        "batch",
    )
    return (
        block_out,
        grad_tokens,
        grad_w_in,
        grad_w_forget,
        grad_b_forget,
        grad_rotation,
        grad_w_outgate,
        grad_gn_gain,
        grad_w_out,
        grad_rms_gain,
        grad_w_gate,
        grad_w_up,
        grad_w_down,
    )


def solution(mesh):
    in_specs = (
        P(("batch", "chan"), None),
        P(None, "chan"),
        P(None, "chan"),
        P("chan"),
        P("chan"),
        P(None, "chan"),
        P("chan"),
        P("chan", None),
        P(),
        P(None, "chan"),
        P(None, "chan"),
        P("chan", None),
        P(("batch", "chan"), None),
        P("batch"),
        P("batch", None),
    )
    out_specs = (
        P(("batch", "chan"), None),
        P(("batch", "chan"), None),
        P(None, "chan"),
        P(None, "chan"),
        P("chan"),
        P("chan"),
        P(None, "chan"),
        P("chan"),
        P("chan", None),
        P("chan"),
        P(None, "chan"),
        P(None, "chan"),
        P("chan", None),
    )
    return jax.shard_map(local, mesh=mesh, in_specs=in_specs, out_specs=out_specs, check_vma=False)
```

profile of v0, /device:TPU:0, one launch (start us, length us, event | category | flops | bytes accessed | tf_op | source)
XLA Modules:
  0.0 1934.3 jit_solution(1145760804688654371)
XLA Ops:
  9.1 118.6 %all-gather.5.cloned.1.call-done = bf16[4096,768]{1,0:T(8,128)(2,1)} async-done(((bf16[1024,768]{1,0:T(8,128)(2,1)}), bf16[4096,768]{1,0:T(8,128)(2,1)}) %all-gather.5.cloned.1.call-update) | async-done | bytes 6291472 | tf_op jit(solution)/shard_map/all_gather | solution.py:144
  127.7 5.4 convolution_bitcast_fusion
  133.1 3.8 fusion.19
  137.5 3.4 subtract_multiply_fusion.6
  184.4 3.2 slice.787
  190.8 3.2 slice.780
  247.3 3.9 bitcast_add_fusion.1
  253.9 3.2 slice.894
  454.2 3.7 pad.1088
  459.5 3.8 pad.1086
  463.2 3.7 pad.1303
  468.7 3.8 pad.1304
  487.9 4.5 multiply_subtract_fusion
  497.5 5.9 add.2354
  503.4 6.5 copy.1181
  509.9 9.1 sub.914
  519.1 7.4 copy.1180
  536.8 6.5 fusion.237
  543.4 210.2 %reduce-scatter.5.cloned.1.call-done = f32[1024,768]{1,0:T(8,128)} async-done(((f32[4096,768]{1,0:T(8,128)}), f32[1024,768]{1,0:T(8,128)}) %reduce-scatter.5.cloned.1.call-update) | async-done | bytes 3145744 | tf_op jit(solution)/shard_map/reduce_scatter | solution.py:163
  761.9 113.7 %all-gather.7.cloned.1.call-done = bf16[4096,768]{1,0:T(8,128)(2,1)} async-done(((bf16[1024,768]{1,0:T(8,128)(2,1)}), bf16[4096,768]{1,0:T(8,128)(2,1)}) %all-gather.7.cloned.1.call-update) | async-done | bytes 6291472 | tf_op jit(solution)/shard_map/all_gather | solution.py:173
  875.6 9.2 fusion.365
  884.8 5.5 fusion.364
  890.3 100.3 %all-gather.9.cloned.1.call-done = bf16[4096,768]{1,0:T(8,128)(2,1)} async-done(((bf16[1024,768]{1,0:T(8,128)(2,1)}), bf16[4096,768]{1,0:T(8,128)(2,1)}) %all-gather.9.cloned.1.call-update) | async-done | bytes 6291472 | tf_op jit(solution)/shard_map/all_gather | solution.py:187
  990.7 11.8 multiply_convert_fusion
  1002.5 3.5 fusion.366
  1005.9 5.5 add_convert_fusion
  1011.5 109.1 %reduce-scatter.9.cloned.1.call-done = bf16[1024,768]{1,0:T(8,128)(2,1)} async-done(((bf16[4096,768]{1,0:T(8,128)(2,1)}), bf16[1024,768]{1,0:T(8,128)(2,1)}) %reduce-scatter.9.cloned.1.call-update) | async-done | bytes 1572880 | tf_op jit(solution)/shard_map/reduce_scatter | solution.py:195
  1120.6 4.2 fusion.7
  1124.8 3.3 fusion.238
  1128.6 8.1 convolution_convert_fusion.1
  1136.8 107.4 %all-gather.11.cloned.1.call-done = bf16[4096,768]{1,0:T(8,128)(2,1)} async-done(((bf16[1024,768]{1,0:T(8,128)(2,1)}), bf16[4096,768]{1,0:T(8,128)(2,1)}) %all-gather.11.cloned.1.call-update) | async-done | bytes 6291472 | tf_op jit(solution)/shard_map/all_gather | solution.py:204
  1244.1 6.8 multiply_reduce_fusion
  1258.5 7.1 copy.1185
  1265.7 9.1 unstack.401
  1277.5 7.2 copy.1182
  1284.7 9.0 unstack.397
  1296.7 6.3 multiply_add_fusion.1
  1303.7 3.2 slice.899
  1310.3 3.2 slice.901
  1318.2 3.2 slice.904
  1323.1 3.7 pad.970
  1339.0 3.7 pad.1011
  1342.8 3.9 pad.833
  1346.7 3.7 pad.936
  1595.8 3.9 pad.937
  1599.7 3.8 pad.928
  1605.2 3.8 pad.933
  1608.9 3.8 pad.1012
  1612.7 3.7 pad.938
  1616.4 3.8 pad.1009
  1620.2 3.8 pad.1013
  1623.9 3.8 pad.1010
  1682.9 5.2 multiply_reduce_fusion.5
  1690.5 5.1 fusion.13
  1698.4 5.4 convolution_convert_fusion
  1703.9 7.5 fusion.369
  1711.4 6.9 fusion.368
  1718.4 4.4 fusion.367
  1722.9 3.2 convolution_bitcast_fusion.1
  1732.1 10.7 all-reduce.223
  1742.9 12.9 all-reduce.224
  1755.8 58.4 %reduce-scatter.11.cloned.1.call-done = bf16[1024,768]{1,0:T(8,128)(2,1)} async-done(((bf16[4096,768]{1,0:T(8,128)(2,1)}), bf16[1024,768]{1,0:T(8,128)(2,1)}) %reduce-scatter.11.cloned.1.call-update) | async-done | bytes 1572880 | tf_op jit(solution)/shard_map/reduce_scatter | solution.py:215
  1814.2 5.0 convert_add_fusion
  1819.1 99.0 %all-reduce.228.cloned.1.call-done = (f32[768,192]{0,1:T(8,128)}, f32[768,96]{0,1:T(8,128)}, f32[768,192]{0,1:T(8,128)}, f32[192,768]{1,0:T(8,128)}, f32[768,384...) async-done(((f32[768,192]{0,1:T(8,128)}, f32[768,96]{0,1:T(8,128)}, f32[768,192]{0,1:T(8,128)}, f32[192,768]{1,0:T(8,128)}, f32[768,384]{1,0:T(8,128)}, ...) | async-done | bytes 5603344 | tf_op jit(solution)/shard_map/psum | solution.py:235
  (1256 shorter events, 698.6 us)
Async XLA Ops:
  7.2 983.5 %copy-start = (bf16[384,768]{1,0:T(8,128)(2,1)S(1)}, bf16[384,768]{1,0:T(8,128)(2,1)}, u32[]{:S(2)}) copy-start(bf16[384,768]{1,0:T(8,128)(2,1)} %param.26) | copy-start | bytes 1769476
  7.2 120.5 %all-gather.5.cloned.1.call-start = ((), (), s32[]{:S(2)}) async-start(), calls=%async_computation.4 | async-start | bytes 7864320 | tf_op jit(solution)/shard_map/all_gather | solution.py:144
  8.0 745.6 %reduce-scatter.5.cloned.1.call-start = ((), (), s32[]{:S(2)}) async-start(), calls=%async_computation.5 | async-start | bytes 15728640 | tf_op jit(solution)/shard_map/reduce_scatter | solution.py:163
  8.9 128.3 %copy-start.337 = (f32[4096]{0:T(1024)}, f32[4096]{0:T(1024)S(1)}, u32[]{:S(2)}) copy-start(f32[4096]{0:T(1024)S(1)} %convert_subtract_fusion) | copy-start | bytes 49156
  9.0 124.1 %copy-start.340 = (bf16[768,480]{0,1:T(8,128)(2,1)}, bf16[768,480]{0,1:T(8,128)(2,1)S(1)}, u32[]{:S(2)}) copy-start(bf16[768,480]{0,1:T(8,128)(2,1)S(1)} %constant_dynamic-update-slice_fusion) | copy-start | bytes 2211844
  9.1 128.1 %copy-start.346 = (f32[96]{0:T(128)}, f32[96]{0:T(128)S(1)}, u32[]{:S(2)}) copy-start(f32[96]{0:T(128)S(1)} %get-tuple-element.705) | copy-start | bytes 1156
  9.1 128.1 %copy-start.348 = (f32[96]{0:T(128)}, f32[96]{0:T(128)S(1)}, u32[]{:S(2)}) copy-start(f32[96]{0:T(128)S(1)} %get-tuple-element.706) | copy-start | bytes 1156
  157.0 322.8 %copy-start.38 = (f32[256,1,96]{0,2,1:T(8,128)}, f32[256,1,96]{0,2,1:T(8,128)S(1)}, u32[]{:S(2)}) copy-start(f32[256,1,96]{0,2,1:T(8,128)S(1)} %copy.1258) | copy-start | bytes 294916
  157.1 321.9 %copy-start.36 = (f32[256,1,96]{0,2,1:T(8,128)}, f32[256,1,96]{0,2,1:T(8,128)S(1)}, u32[]{:S(2)}) copy-start(f32[256,1,96]{0,2,1:T(8,128)S(1)} %copy.1254) | copy-start | bytes 294916
  157.2 321.0 %copy-start.34 = (f32[256,1,96]{0,2,1:T(8,128)}, f32[256,1,96]{0,2,1:T(8,128)S(1)}, u32[]{:S(2)}) copy-start(f32[256,1,96]{0,2,1:T(8,128)S(1)} %copy.1250) | copy-start | bytes 294916
  157.3 320.1 %copy-start.32 = (f32[256,1,96]{0,2,1:T(8,128)}, f32[256,1,96]{0,2,1:T(8,128)S(1)}, u32[]{:S(2)}) copy-start(f32[256,1,96]{0,2,1:T(8,128)S(1)} %copy.1246) | copy-start | bytes 294916
  165.4 16.0 copy-start.43
  165.4 16.0 copy-start.46
  166.6 17.7 copy-start.111
  167.6 16.7 copy-start.107
  198.4 16.7 copy-start.294
  223.8 23.3 %copy-start.41 = (f32[256,1,96]{0,2,1:T(8,128)S(1)}, f32[256,1,96]{0,2,1:T(8,128)}, u32[]{:S(2)}) copy-start(f32[256,1,96]{0,2,1:T(8,128)} %copy-done.40) | copy-start | bytes 294916
  223.8 23.3 %copy-start.44 = (f32[256,1,96]{0,2,1:T(8,128)S(1)}, f32[256,1,96]{0,2,1:T(8,128)}, u32[]{:S(2)}) copy-start(f32[256,1,96]{0,2,1:T(8,128)} %copy.1262) | copy-start | bytes 294916
  223.8 23.3 %copy-start.47 = (f32[256,1,96]{0,2,1:T(8,128)S(1)}, f32[256,1,96]{0,2,1:T(8,128)}, u32[]{:S(2)}) copy-start(f32[256,1,96]{0,2,1:T(8,128)} %copy.1266) | copy-start | bytes 294916
  223.8 23.3 %copy-start.50 = (f32[256,1,96]{0,2,1:T(8,128)S(1)}, f32[256,1,96]{0,2,1:T(8,128)}, u32[]{:S(2)}) copy-start(f32[256,1,96]{0,2,1:T(8,128)} %copy-done.49) | copy-start | bytes 294916
  223.9 23.3 %copy-start.53 = (f32[256,1,96]{0,2,1:T(8,128)S(1)}, f32[256,1,96]{0,2,1:T(8,128)}, u32[]{:S(2)}) copy-start(f32[256,1,96]{0,2,1:T(8,128)} %copy.1270) | copy-start | bytes 294916
  223.9 23.3 %copy-start.56 = (f32[256,1,96]{0,2,1:T(8,128)S(1)}, f32[256,1,96]{0,2,1:T(8,128)}, u32[]{:S(2)}) copy-start(f32[256,1,96]{0,2,1:T(8,128)} %copy-done.55) | copy-start | bytes 294916
  223.9 23.3 %copy-start.60 = (f32[256,1,96]{0,2,1:T(8,128)S(1)}, f32[256,1,96]{0,2,1:T(8,128)}, u32[]{:S(2)}) copy-start(f32[256,1,96]{0,2,1:T(8,128)} %copy.1274) | copy-start | bytes 294916
  223.9 23.3 %copy-start.64 = (f32[256,1,96]{0,2,1:T(8,128)S(1)}, f32[256,1,96]{0,2,1:T(8,128)}, u32[]{:S(2)}) copy-start(f32[256,1,96]{0,2,1:T(8,128)} %copy-done.63) | copy-start | bytes 294916
  223.9 23.3 %copy-start.68 = (f32[256,1,96]{0,2,1:T(8,128)S(1)}, f32[256,1,96]{0,2,1:T(8,128)}, u32[]{:S(2)}) copy-start(f32[256,1,96]{0,2,1:T(8,128)} %copy.1278) | copy-start | bytes 294916
  223.9 23.3 %copy-start.72 = (f32[256,1,96]{0,2,1:T(8,128)S(1)}, f32[256,1,96]{0,2,1:T(8,128)}, u32[]{:S(2)}) copy-start(f32[256,1,96]{0,2,1:T(8,128)} %copy-done.71) | copy-start | bytes 294916
  223.9 23.3 %copy-start.76 = (f32[256,1,96]{0,2,1:T(8,128)S(1)}, f32[256,1,96]{0,2,1:T(8,128)}, u32[]{:S(2)}) copy-start(f32[256,1,96]{0,2,1:T(8,128)} %copy.1282) | copy-start | bytes 294916
  223.9 23.3 %copy-start.80 = (f32[256,1,96]{0,2,1:T(8,128)S(1)}, f32[256,1,96]{0,2,1:T(8,128)}, u32[]{:S(2)}) copy-start(f32[256,1,96]{0,2,1:T(8,128)} %copy-done.79) | copy-start | bytes 294916
  223.9 23.3 %copy-start.84 = (f32[256,1,96]{0,2,1:T(8,128)S(1)}, f32[256,1,96]{0,2,1:T(8,128)}, u32[]{:S(2)}) copy-start(f32[256,1,96]{0,2,1:T(8,128)} %copy.1286) | copy-start | bytes 294916
  223.9 23.3 %copy-start.88 = (f32[256,1,96]{0,2,1:T(8,128)S(1)}, f32[256,1,96]{0,2,1:T(8,128)}, u32[]{:S(2)}) copy-start(f32[256,1,96]{0,2,1:T(8,128)} %copy-done.87) | copy-start | bytes 294916
  224.0 23.3 %copy-start.92 = (f32[256,1,96]{0,2,1:T(8,128)S(1)}, f32[256,1,96]{0,2,1:T(8,128)}, u32[]{:S(2)}) copy-start(f32[256,1,96]{0,2,1:T(8,128)} %copy.1290) | copy-start | bytes 294916
  224.0 23.3 %copy-start.96 = (f32[256,1,96]{0,2,1:T(8,128)S(1)}, f32[256,1,96]{0,2,1:T(8,128)}, u32[]{:S(2)}) copy-start(f32[256,1,96]{0,2,1:T(8,128)} %copy-done.95) | copy-start | bytes 294916
  224.0 23.3 %copy-start.100 = (f32[256,1,96]{0,2,1:T(8,128)S(1)}, f32[256,1,96]{0,2,1:T(8,128)}, u32[]{:S(2)}) copy-start(f32[256,1,96]{0,2,1:T(8,128)} %copy-done.99) | copy-start | bytes 294916
  224.0 23.3 %copy-start.104 = (f32[256,1,96]{0,2,1:T(8,128)S(1)}, f32[256,1,96]{0,2,1:T(8,128)}, u32[]{:S(2)}) copy-start(f32[256,1,96]{0,2,1:T(8,128)} %copy-done.103) | copy-start | bytes 294916
  224.0 23.3 %copy-start.108 = (f32[256,1,96]{0,2,1:T(8,128)S(1)}, f32[256,1,96]{0,2,1:T(8,128)}, u32[]{:S(2)}) copy-start(f32[256,1,96]{0,2,1:T(8,128)} %copy-done.107) | copy-start | bytes 294916
  224.0 23.3 %copy-start.112 = (f32[256,1,96]{0,2,1:T(8,128)S(1)}, f32[256,1,96]{0,2,1:T(8,128)}, u32[]{:S(2)}) copy-start(f32[256,1,96]{0,2,1:T(8,128)} %copy-done.111) | copy-start | bytes 294916
  224.0 23.3 %copy-start.116 = (f32[256,1,96]{0,2,1:T(8,128)S(1)}, f32[256,1,96]{0,2,1:T(8,128)}, u32[]{:S(2)}) copy-start(f32[256,1,96]{0,2,1:T(8,128)} %copy.1237) | copy-start | bytes 294916
  251.3 24.0 %copy-start.256 = (f32[128,96]{0,1:T(8,128)S(1)}, f32[128,96]{0,1:T(8,128)}, u32[]{:S(2)}) copy-start(f32[128,96]{0,1:T(8,128)} %slice.787) | copy-start | bytes 147460
  251.3 24.0 %copy-start.306 = (f32[128,96]{0,1:T(8,128)S(1)}, f32[128,96]{0,1:T(8,128)}, u32[]{:S(2)}) copy-start(f32[128,96]{0,1:T(8,128)} %slice.780) | copy-start | bytes 147460
  253.9 27.1 %copy-start.257 = (f32[128,96]{0,1:T(8,128)}, f32[128,96]{0,1:T(8,128)S(1)}, u32[]{:S(2)}) copy-start(f32[128,96]{0,1:T(8,128)S(1)} %slice.781) | copy-start | bytes 147460
  267.1 23.5 %copy-start.258 = (f32[128,96]{0,1:T(8,128)}, f32[128,96]{0,1:T(8,128)S(1)}, u32[]{:S(2)}) copy-start(f32[128,96]{0,1:T(8,128)S(1)} %slice.788) | copy-start | bytes 147460
  268.8 18.7 copy-start.307
  270.7 21.6 %copy-start.259 = (f32[128,96]{0,1:T(8,128)}, f32[128,96]{0,1:T(8,128)S(1)}, u32[]{:S(2)}) copy-start(f32[128,96]{0,1:T(8,128)S(1)} %slice.784) | copy-start | bytes 147460
  275.3 21.5 %copy-start.141 = (f32[128,96]{0,1:T(8,128)}, f32[128,96]{0,1:T(8,128)S(1)}, u32[]{:S(2)}) copy-start(f32[128,96]{0,1:T(8,128)S(1)} %get-tuple-element.639) | copy-start | bytes 147460
  275.3 21.5 %copy-start.143 = (f32[128,96]{0,1:T(8,128)}, f32[128,96]{0,1:T(8,128)S(1)}, u32[]{:S(2)}) copy-start(f32[128,96]{0,1:T(8,128)S(1)} %get-tuple-element.638) | copy-start | bytes 147460
  276.2 20.1 %copy-start.260 = (f32[64,96]{0,1:T(8,128)}, f32[64,96]{0,1:T(8,128)S(1)}, u32[]{:S(2)}) copy-start(f32[64,96]{0,1:T(8,128)S(1)} %slice.797) | copy-start | bytes 73732
  311.4 43.7 %copy-start.126 = (f32[4,96]{0,1:T(8,128)}, f32[4,96]{0,1:T(8,128)S(1)}, u32[]{:S(2)}) copy-start(f32[4,96]{0,1:T(8,128)S(1)} %get-tuple-element.628) | copy-start | bytes 4612
  373.6 34.4 %copy-start.147 = (f32[32,96]{0,1:T(8,128)S(1)}, f32[32,96]{0,1:T(8,128)}, u32[]{:S(2)}) copy-start(f32[32,96]{0,1:T(8,128)} %copy-done.146) | copy-start | bytes 36868
  411.8 32.5 %copy-start.142 = (f32[128,96]{0,1:T(8,128)S(1)}, f32[128,96]{0,1:T(8,128)}, u32[]{:S(2)}) copy-start(f32[128,96]{0,1:T(8,128)} %copy-done.141) | copy-start | bytes 147460
  451.2 24.3 %copy-start.325 = (f32[127,96]{0,1:T(8,128)}, f32[127,96]{0,1:T(8,128)S(1)}, u32[]{:S(2)}) copy-start(f32[127,96]{0,1:T(8,128)S(1)} %get-tuple-element.198) | copy-start | bytes 146308
  509.9 16.5 copy-start.16
  543.3 210.3 %copy-start.29 = (bf16[1024,768]{1,0:T(8,128)(2,1)S(1)}, bf16[1024,768]{1,0:T(8,128)(2,1)}, u32[]{:S(2)}) copy-start(bf16[1024,768]{1,0:T(8,128)(2,1)} %param.15) | copy-start | bytes 4718596
  543.3 214.2 %copy-start.342 = (f32[768]{0:T(1024)S(1)}, f32[768]{0:T(1024)}, u32[]{:S(2)}) copy-start(f32[768]{0:T(1024)} %param.23) | copy-start | bytes 9220
  543.3 332.3 %all-gather.7.cloned.1.call-start = ((), (), s32[]{:S(2)}) async-start(), calls=%async_computation.6 | async-start | bytes 7864320 | tf_op jit(solution)/shard_map/all_gather | solution.py:173
  759.1 231.6 %all-gather.9.cloned.1.call-start = ((), (), s32[]{:S(2)}) async-start(), calls=%async_computation.8 | async-start | bytes 7864320 | tf_op jit(solution)/shard_map/all_gather | solution.py:187
  761.8 113.8 %copy-start.291 = (bf16[768,384]{1,0:T(8,128)(2,1)S(1)}, bf16[768,384]{1,0:T(8,128)(2,1)}, u32[]{:S(2)}) copy-start(bf16[768,384]{1,0:T(8,128)(2,1)} %param.25) | copy-start | bytes 1769476
  761.8 123.0 %copy-start.286 = (bf16[768,384]{1,0:T(8,128)(2,1)S(1)}, bf16[768,384]{1,0:T(8,128)(2,1)}, u32[]{:S(2)}) copy-start(bf16[768,384]{1,0:T(8,128)(2,1)} %param.24) | copy-start | bytes 1769476
  761.8 358.7 %reduce-scatter.9.cloned.1.call-start = ((), (), s32[]{:S(2)}) async-start(), calls=%async_computation.9 | async-start | bytes 7864320 | tf_op jit(solution)/shard_map/reduce_scatter | solution.py:195
  1011.4 232.7 %all-gather.11.cloned.1.call-start = ((), (), s32[]{:S(2)}) async-start(), calls=%async_computation.10 | async-start | bytes 7864320 | tf_op jit(solution)/shard_map/all_gather | solution.py:204
  1128.1 627.6 %reduce-scatter.7.cloned.1.call-start = ((), (), s32[]{:S(2)}) async-start(), calls=%async_computation.7 | async-start | bytes 7864320 | tf_op jit(solution)/shard_map/reduce_scatter | solution.py:180
  1136.7 677.4 %reduce-scatter.11.cloned.1.call-start = ((), (), s32[]{:S(2)}) async-start(), calls=%async_computation.11 | async-start | bytes 7864320 | tf_op jit(solution)/shard_map/reduce_scatter | solution.py:215
  1703.8 214.4 %all-reduce.228.cloned.1.call-start = ((), (), s32[]{:S(2)}) async-start(), calls=%async_computation.12 | async-start | bytes 11206656 | tf_op jit(solution)/shard_map/psum | solution.py:235
  1703.8 19.0 slice-start.2
  1730.2 83.9 %copy-start.4 = (f32[1024,768]{1,0:T(8,128)S(1)}, f32[1024,768]{1,0:T(8,128)}, u32[]{:S(2)}) copy-start(f32[1024,768]{1,0:T(8,128)} %copy-done.2) | copy-start | bytes 9437188
  (308 other events, 1349.8 us)
Sparse Core Ops, SparseCore 0:
  9.6 118.0 all-gather.4
  543.4 210.0 reduce-scatter.4
  759.2 116.3 all-gather.6
  877.0 113.5 all-gather.8
  1011.6 108.9 reduce-scatter.8
  1128.2 115.8 all-gather.10
  1246.4 108.9 reduce-scatter.6
  1703.9 110.2 reduce-scatter.10
  1819.6 98.5 all-reduce.227
where the time goes:
time: 1960 us; the launch traced here: 1930 us
  waiting for transfers between devices  918 us (47%)
  local copies, waits for them, and re-layouts  663 us (34%)
  other arithmetic  217 us (11%)
  matrix products  92 us (5%)
  blocking collectives  23.5 us (1%)
  between operations  20.3 us (1%)
    pad x118, local copies, waits for them, and re-layouts, recurrence(): lax.associative_scan(complex_combine, (prod_real, prod_imag, state_real,...  270 us
    reduce_scatter x1, waiting for transfers between devices, local(): lax.psum_scatter(jnp.dot(mix_low, w_out, preferred_element_type=jnp.float...  210 us
    slice x111, local copies, waits for them, and re-layouts, recurrence(): lax.associative_scan(complex_combine, (prod_real, prod_imag, state_real,...  127 us
    unnamed x815, local copies, waits for them, and re-layouts  125 us
    all_gather x1, waiting for transfers between devices, local(): all_tokens = lax.all_gather(tokens, 'chan', axis=0, tiled=True)  119 us
    all_gather x1, waiting for transfers between devices, local(): norm_all = lax.all_gather(ffn_in, 'chan', axis=0, tiled=True)  114 us
    reduce_scatter x1, waiting for transfers between devices, local(): lax.psum_scatter((contract(d_gate, w_gate, 1, 1) + contract(d_up, w_up, 1...  109 us
    all_gather x1, waiting for transfers between devices, local(): d_mixed_all = lax.all_gather(d_mixed_low, 'chan', axis=0, tiled=True)  107 us
  transfers between devices with their start and end apart: 9, of which 8 were waited for; matrix products, arithmetic and copies ran while one was open for 26% of the time, Pallas kernels for 0%

commit v1 on v0

v1 whole, which is shorter than its diff:
```python
import functools

import jax
import jax.numpy as jnp
from jax import lax
from jax.experimental import pallas as pl
from jax.experimental.pallas import tpu as pltpu
from jax.sharding import PartitionSpec as P

MESH = pl.DeviceIdType.MESH
BF = jnp.bfloat16
F32 = jnp.float32
HEAD_CH = 32
SEGS = 16
TM = 256
MT0, WO0, WG0, WD0, PIECE = 0, 512, 704, 1472, 1856
PAD0 = 480


def dot(left, right, left_dim, right_dim):
    return lax.dot_general(
        left, right, (((left_dim,), (right_dim,)), ((), ())), preferred_element_type=F32
    )


def rows_of(tile, size):
    return pl.ds(pl.multiple_of(tile * size, size), size)


def sigmoid(v):
    return 1.0 / (1.0 + jnp.exp(-v))


def get(ref, rows, first, count):
    return jnp.concatenate([ref[first + k, rows, :] for k in range(count)], axis=1)


def put(ref, rows, first, v):
    for k in range(v.shape[1] // 128):
        ref[first + k, rows, :] = v[:, 128 * k : 128 * (k + 1)]


def fold_rows(v):
    return jnp.sum(v.reshape(v.shape[0] // 8, 8, v.shape[1]), axis=0)


def main_kernel(
    w_hbm, tok_hbm, cot_hbm, par_ref, rms_ref, bucket_ref, len_ref,
    g_hbm, gtok_hbm, out_hbm,
    w, tok, sd, pv, om, pg, ws, xh, rstd, res, fin, mix, out, dff, hid, dgu, dm, dp,
    ones, parx, carx, carb, seg, sgrad, seg_prod,
    load_sem, store_sem, par_send, par_recv, car_send, car_recv, cab_send, cab_recv,
):
    n_chan, n_rows = 4, tok.shape[0]
    width = tok.shape[1]
    half = width // 2
    lt = half // 128
    n_tiles = n_rows // TM
    seg_len = n_rows // SEGS
    b = lax.axis_index("batch")
    c = lax.axis_index("chan")
    peers = [lax.rem(c + j, n_chan) for j in range(1, n_chan)]

    loads = [
        pltpu.make_async_copy(tok_hbm, tok, load_sem.at[0]),
        pltpu.make_async_copy(w_hbm, w, load_sem.at[1]),
        pltpu.make_async_copy(cot_hbm, sd, load_sem.at[2]),
    ]
    for load in loads:
        load.start()

    barrier = pltpu.get_barrier_semaphore()
    for peer in peers:
        pl.semaphore_signal(barrier, inc=1, device_id=(b, peer), device_id_type=MESH)
    pl.semaphore_wait(barrier, n_chan - 1)

    def exchange(ref, send_sem, recv_sem):
        copies = [
            pltpu.make_async_remote_copy(
                ref.at[c], ref.at[c], send_sem.at[j], recv_sem.at[j],
                device_id=(b, peer), device_id_type=MESH,
            )
            for j, peer in enumerate(peers)
        ]
        return copies

    parx[c] = par_ref[...]
    par_copies = exchange(parx, par_send, par_recv)
    for copy in par_copies:
        copy.start()
    lane_r = lax.broadcasted_iota(jnp.int32, (half, half), 0) // HEAD_CH
    lane_c = lax.broadcasted_iota(jnp.int32, (half, half), 1) // HEAD_CH
    ones[...] = jnp.where(lane_r == lane_c, 1.0 / (2 * HEAD_CH), 0.0).astype(BF)
    sgrad[...] = jnp.zeros_like(sgrad)

    def head_mean(v):
        high = v.astype(BF)
        low = (v - high.astype(F32)).astype(BF)
        return dot(high, ones[...], 1, 0) + dot(low, ones[...], 1, 0)

    bucket = bucket_ref[0]
    base = c * n_rows
    offset = jnp.bitwise_and(base, bucket - 1)
    slot_limit = len_ref[0, 0]
    for k in range(1, len_ref.shape[1]):
        slot_limit = jnp.where(base >= k * bucket, len_ref[0, k], slot_limit)
    live_rows = slot_limit - offset
    not_start = jnp.where(offset == 0, 0.0, 1.0).astype(F32)

    for copy in par_copies:
        copy.wait()
    par = parx[0] + parx[1] + parx[2] + parx[3]
    bias = par[0:1, :]
    cos1, sin1 = par[1:2, :], par[2:3, :]
    gain_r, gain_i = par[3:4, :], par[4:5, :]
    rms_gain = rms_ref[...]
    cos16 = jnp.broadcast_to(cos1, (SEGS, half))
    sin16 = jnp.broadcast_to(sin1, (SEGS, half))

    def power(count):
        rr, ri = cos1, sin1
        while count > 1:
            rr, ri = rr * rr - ri * ri, 2.0 * rr * ri
            count //= 2
        return rr, ri

    seg_cos, seg_sin = power(seg_len)
    all_cos, all_sin = power(n_rows)

    loads[0].wait()
    loads[1].wait()

    def section(k):
        return jnp.concatenate(
            [w[cc, 96 * k : 96 * k + 96, :] for cc in range(n_chan)], axis=0
        )

    def out_rows(k):
        return jnp.concatenate(
            [w[cc, WO0 + 96 * k : WO0 + 96 * k + 96, :] for cc in range(n_chan)], axis=0
        )

    @pl.loop(0, n_tiles)
    def _(i):
        rows = rows_of(i, TM)
        x = tok[rows, :]
        for k in range(2):
            pre = dot(x, section(k), 1, 1)
            pv[rows, k * half : (k + 1) * half] = pre
            put(out, rows, k * lt, pre * sigmoid(pre))
        put(om, rows, 0, 1.0 / (1.0 + jnp.exp(dot(x, section(2), 1, 1) + bias)))

    def strided(t):
        return pl.ds(t, SEGS, stride=seg_len)

    def first(t, carry):
        sr, si, prod = carry
        o = get(om, strided(t), 0, lt)
        f = 1.0 - o
        vr = get(out, strided(t), 0, lt)
        vi = get(out, strided(t), lt, lt)
        tr = cos16 * sr - sin16 * si
        ti = sin16 * sr + cos16 * si
        return f * tr + o * vr, f * ti + o * vi, prod * f

    zero = jnp.zeros((SEGS, half), F32)
    end_r, end_i, prod = lax.fori_loop(
        0, seg_len, first, (zero, zero, jnp.ones((SEGS, half), F32)), unroll=4
    )
    seg[0] = end_r
    seg[1] = end_i
    seg_prod[...] = prod

    def fold_forward(cr, ci, keep):
        total = jnp.ones((1, half), F32)
        for s in range(SEGS):
            if keep:
                seg[2, s : s + 1, :] = cr
                seg[3, s : s + 1, :] = ci
            p = seg_prod[s : s + 1, :]
            ar, ai = p * seg_cos, p * seg_sin
            cr, ci = (
                ar * cr - ai * ci + seg[0, s : s + 1, :],
                ar * ci + ai * cr + seg[1, s : s + 1, :],
            )
            total = total * p
        return cr, ci, total

    zrow = jnp.zeros((1, half), F32)
    er, ei, total = fold_forward(zrow, zrow, False)
    carx[c, 0:1, :] = er
    carx[c, 1:2, :] = ei
    carx[c, 2:3, :] = total * all_cos * not_start
    carx[c, 3:4, :] = total * all_sin * not_start
    car_copies = exchange(carx, car_send, car_recv)
    for copy in car_copies:
        copy.start()

    @pl.loop(0, n_tiles)
    def _(i):
        rows = rows_of(i, TM)
        x = tok[rows, :]
        for k in range(2):
            pg[rows, k * half : (k + 1) * half] = dot(x, section(3 + k), 1, 1)

    for copy in car_copies:
        copy.wait()
    cr, ci = zrow, zrow
    for k in range(n_chan - 1):
        ar, ai = carx[k, 2:3, :], carx[k, 3:4, :]
        nr = ar * cr - ai * ci + carx[k, 0:1, :]
        ni = ar * ci + ai * cr + carx[k, 1:2, :]
        cr = jnp.where(k < c, nr, cr)
        ci = jnp.where(k < c, ni, ci)
    fold_forward(cr * not_start, ci * not_start, True)

    def second(t, carry):
        sr, si = carry
        o = get(om, strided(t), 0, lt)
        f = 1.0 - o
        vr = get(out, strided(t), 0, lt)
        vi = get(out, strided(t), lt, lt)
        tr = cos16 * sr - sin16 * si
        ti = sin16 * sr + cos16 * si
        put(ws, strided(t), 0, tr)
        put(ws, strided(t), lt, ti)
        return f * tr + o * vr, f * ti + o * vi

    lax.fori_loop(0, seg_len, second, (seg[2], seg[3]), unroll=4)

    @pl.loop(0, n_tiles)
    def _(i):
        rows = rows_of(i, TM)
        o = get(om, rows, 0, lt)
        f = 1.0 - o
        gr, gi = pg[rows, :half], pg[rows, half:]
        yr = gr * sigmoid(gr) * (f * get(ws, rows, 0, lt) + o * get(out, rows, 0, lt))
        yi = gi * sigmoid(gi) * (f * get(ws, rows, lt, lt) + o * get(out, rows, lt, lt))
        mean = head_mean(yr + yi)
        yr, yi = yr - mean, yi - mean
        inv = lax.rsqrt(head_mean(yr * yr + yi * yi) + 1e-5)
        yr, yi = yr * inv, yi * inv
        rstd[rows, :] = inv
        xh[rows, :half] = yr
        xh[rows, half:] = yi
        lr, li = (yr * gain_r).astype(BF), (yi * gain_i).astype(BF)
        mix[rows, :half] = lr
        mix[rows, half:] = li
        r = tok[rows, :].astype(F32) + (
            dot(lr, out_rows(0), 1, 0) + dot(li, out_rows(1), 1, 0)
        )
        res[rows, :] = r
        put(out, rows, 0, r)
        rinv = lax.rsqrt(jnp.mean(r * r, axis=1, keepdims=True) + 1e-6)
        fin[rows, :] = (r * rinv * rms_gain).astype(BF)
        dff[rows, :] = jnp.zeros((TM, width), F32)

    loads[2].wait()

    @pl.loop(0, n_tiles)
    def _(i):
        rows = rows_of(i, TM)
        place = lax.broadcasted_iota(jnp.int32, (TM, 1), 0) + i * TM
        live = jnp.where(place < live_rows, 1.0, 0.0)
        sd[rows, :] = (sd[rows, :].astype(F32) * live).astype(BF)

    hw = hid.shape[1]

    @pl.loop(0, n_chan)
    def _(j):
        cc = lax.rem(c + j, n_chan)

        @pl.loop(0, n_tiles)
        def _(i):
            rows = rows_of(i, TM)
            gate_up = dot(fin[rows, :], w[cc, WG0:WD0, :], 1, 1)
            d_hid = dot(sd[rows, :], w[cc, WD0:PIECE, :], 1, 1)
            gate, up = gate_up[:, :hw], gate_up[:, hw:]
            sig = sigmoid(gate)
            act = gate * sig
            h = (act * up).astype(BF)
            hid[rows, :] = h
            dg = (d_hid * up * (sig + act * (1.0 - sig))).astype(BF)
            du = (d_hid * act).astype(BF)
            dgu[rows, :hw] = dg
            dgu[rows, hw:] = du
            put(out, rows, 0, get(out, rows, 0, 2 * lt) + dot(h, w[cc, WD0:PIECE, :], 1, 0))
            dff[rows, :] += dot(dgu[rows, :], w[cc, WG0:WD0, :], 1, 0)

        for k in range(2):
            w[cc, WG0 + hw * k : WG0 + hw * (k + 1), :] = dot(
                dgu[:, hw * k : hw * (k + 1)], fin[...], 0, 0
            ).astype(BF)
        w[cc, WD0:PIECE, :] = dot(hid[...], sd[...], 0, 0).astype(BF)

    @pl.loop(0, n_tiles)
    def _(i):
        rows = rows_of(i, TM)
        fin[rows, :] = get(out, rows, 0, 2 * lt).astype(BF)
        r = res[rows, :]
        rinv = lax.rsqrt(jnp.mean(r * r, axis=1, keepdims=True) + 1e-6)
        rhat = r * rinv
        d = dff[rows, :]
        sgrad[2] += fold_rows(d * rhat)
        t = d * rms_gain
        dres = sd[rows, :].astype(F32) + rinv * (
            t - rhat * jnp.mean(t * rhat, axis=1, keepdims=True)
        )
        dff[rows, :] = dres
        low = dres.astype(BF)
        dm[rows, :] = low
        dr = dot(low, out_rows(0), 1, 1)
        di = dot(low, out_rows(1), 1, 1)
        xr, xi = xh[rows, :half], xh[rows, half:]
        sgrad[1, :, :half] += fold_rows(dr * xr)
        sgrad[1, :, half:] += fold_rows(di * xi)
        dr, di = dr * gain_r, di * gain_i
        m1 = head_mean(dr + di)
        m2 = head_mean(dr * xr + di * xi)
        inv = rstd[rows, :]
        dr = inv * (dr - m1 - xr * m2)
        di = inv * (di - m1 - xi * m2)
        o = get(om, rows, 0, lt)
        f = 1.0 - o
        for k, dy in ((0, dr), (1, di)):
            cols = slice(k * half, (k + 1) * half)
            pre = pv[rows, cols]
            state = f * get(ws, rows, k * lt, lt) + o * (pre * sigmoid(pre))
            g = pg[rows, cols]
            sig = sigmoid(g)
            act = g * sig
            dp[rows, (3 + k) * half : (4 + k) * half] = (
                dy * state * (sig + act * (1.0 - sig))
            ).astype(BF)
            put(out, rows, k * lt, dy * act)

    out_copy = pltpu.make_async_copy(fin, out_hbm, store_sem.at[0])
    out_copy.start()

    def first_back(k, carry):
        qr, qi = carry
        t = seg_len - 1 - k
        f = 1.0 - get(om, strided(t), 0, lt)
        lr = get(out, strided(t), 0, lt) + qr
        li = get(out, strided(t), lt, lt) + qi
        return f * (cos16 * lr + sin16 * li), f * (cos16 * li - sin16 * lr)

    qr, qi = lax.fori_loop(0, seg_len, first_back, (zero, zero), unroll=4)
    seg[0] = qr
    seg[1] = qi

    def fold_back(cr, ci, keep):
        for s in range(SEGS - 1, -1, -1):
            if keep:
                seg[2, s : s + 1, :] = cr
                seg[3, s : s + 1, :] = ci
            p = seg_prod[s : s + 1, :]
            ar, ai = p * seg_cos, -(p * seg_sin)
            cr, ci = (
                ar * cr - ai * ci + seg[0, s : s + 1, :],
                ar * ci + ai * cr + seg[1, s : s + 1, :],
            )
        return cr, ci

    er, ei = fold_back(zrow, zrow, False)
    carb[c, 0:1, :] = er * not_start
    carb[c, 1:2, :] = ei * not_start
    car_copies = exchange(carb, cab_send, cab_recv)
    for copy in car_copies:
        copy.start()

    for k in range(2):
        grad = dot(mix[:, k * half : (k + 1) * half], dm[...], 0, 0).astype(BF)
        for cc in range(n_chan):
            w[cc, WO0 + 96 * k : WO0 + 96 * k + 96, :] = grad[96 * cc : 96 * cc + 96, :]

    for copy in car_copies:
        copy.wait()
    cr, ci = zrow, zrow
    for k in range(n_chan - 1, 0, -1):
        ar, ai = carx[k, 2:3, :], -carx[k, 3:4, :]
        nr = ar * cr - ai * ci + carb[k, 0:1, :]
        ni = ar * ci + ai * cr + carb[k, 1:2, :]
        cr = jnp.where(k > c, nr, cr)
        ci = jnp.where(k > c, ni, ci)
    fold_back(cr, ci, True)

    def second_back(k, carry):
        qr, qi = carry
        t = seg_len - 1 - k
        f = 1.0 - get(om, strided(t), 0, lt)
        lr = get(out, strided(t), 0, lt) + qr
        li = get(out, strided(t), lt, lt) + qi
        put(out, strided(t), 0, lr)
        put(out, strided(t), lt, li)
        return f * (cos16 * lr + sin16 * li), f * (cos16 * li - sin16 * lr)

    lax.fori_loop(0, seg_len, second_back, (seg[2], seg[3]), unroll=4)

    @pl.loop(0, n_tiles)
    def _(i):
        rows = rows_of(i, TM)
        o = get(om, rows, 0, lt)
        f = 1.0 - o
        df = jnp.zeros((TM, half), F32)
        for k in range(2):
            cols = slice(k * half, (k + 1) * half)
            pre = pv[rows, cols]
            sig = sigmoid(pre)
            act = pre * sig
            lam = get(out, rows, k * lt, lt)
            df += lam * (get(ws, rows, k * lt, lt) - act)
            dp[rows, cols] = (o * lam * (sig + act * (1.0 - sig))).astype(BF)
        dx = df * f * o
        dp[rows, 2 * half : 3 * half] = dx.astype(BF)
        sgrad[0, :, :half] += fold_rows(dx)
        sgrad[0, :, half:] += fold_rows(
            f
            * (
                get(out, rows, lt, lt) * get(ws, rows, 0, lt)
                - get(out, rows, 0, lt) * get(ws, rows, lt, lt)
            )
        )
        acc = dff[rows, :]
        for k in range(5):
            acc += dot(dp[rows, k * half : (k + 1) * half], section(k), 1, 0)
        dff[rows, :] = acc

    gtok_copy = pltpu.make_async_copy(dff, gtok_hbm, store_sem.at[1])
    gtok_copy.start()

    small = jnp.concatenate(
        [jnp.sum(sgrad[k], axis=0, keepdims=True) for k in range(3)]
        + [jnp.zeros((13, width), F32)],
        axis=0,
    ).astype(BF)
    for cc in range(n_chan):
        w[cc, PAD0 : PAD0 + 16, :] = small
        w[cc, PAD0 + 16 : WO0, :] = jnp.zeros((16, width), BF)
    for k in range(5):
        grad = dot(dp[:, k * half : (k + 1) * half], tok[...], 0, 0).astype(BF)
        for cc in range(n_chan):
            w[cc, 96 * k : 96 * k + 96, :] = grad[96 * cc : 96 * cc + 96, :]

    g_copy = pltpu.make_async_copy(w, g_hbm, store_sem.at[2])
    g_copy.start()
    for copy in (out_copy, gtok_copy, g_copy):
        copy.wait()


def main_call(w_all, tokens, cotangent, params, rms, bucket, lengths):
    rows, width = tokens.shape
    half = width // 2
    n_chan = w_all.shape[0]
    hw = (WD0 - WG0) // 2
    any_spec = pl.BlockSpec(memory_space=pl.ANY)
    vmem = pl.BlockSpec(memory_space=pltpu.VMEM)
    smem = pl.BlockSpec(memory_space=pltpu.SMEM)
    full32 = pltpu.VMEM((rows, width), F32)
    half32 = pltpu.VMEM((rows, half), F32)
    tiles32 = pltpu.VMEM((width // 128, rows, 128), F32)
    full16 = pltpu.VMEM((rows, width), BF)
    return pl.pallas_call(
        main_kernel,
        out_shape=[
            jax.ShapeDtypeStruct(w_all.shape, BF),
            jax.ShapeDtypeStruct((rows, width), F32),
            jax.ShapeDtypeStruct((rows, width), BF),
        ],
        in_specs=[any_spec, any_spec, any_spec, vmem, vmem, smem, smem],
        out_specs=[any_spec] * 3,
        scratch_shapes=[
            pltpu.VMEM(w_all.shape, BF),
            full16, full16, full32, pltpu.VMEM((half // 128, rows, 128), F32), full32, tiles32,
            full32, half32, full32, full16, full16, tiles32, full32,
            pltpu.VMEM((rows, hw), BF), pltpu.VMEM((rows, 2 * hw), BF),
            full16, pltpu.VMEM((rows, 5 * half), BF),
            pltpu.VMEM((half, half), BF),
            pltpu.VMEM((n_chan, 8, half), F32),
            pltpu.VMEM((n_chan, 8, half), F32),
            pltpu.VMEM((n_chan, 8, half), F32),
            pltpu.VMEM((4, SEGS, half), F32),
            pltpu.VMEM((3, 8, width), F32),
            pltpu.VMEM((SEGS, half), F32),
            pltpu.SemaphoreType.DMA((3,)),
            pltpu.SemaphoreType.DMA((3,)),
        ]
        + [pltpu.SemaphoreType.DMA((n_chan - 1,))] * 6,
        compiler_params=pltpu.CompilerParams(
            collective_id=0, has_side_effects=True, vmem_limit_bytes=60 * 2**20
        ),
        cost_estimate=pl.CostEstimate(
            flops=34 * 10**9, bytes_accessed=3 * 10**7, transcendentals=0
        ),
        name="block",
    )(w_all, tokens, cotangent, params, rms, bucket, lengths)


def split_parts(v):
    heads = v.shape[1] // (2 * HEAD_CH)
    return v.T.reshape(heads, 2, HEAD_CH, -1).swapaxes(0, 1).reshape(v.shape[1], -1)


def join_parts(v):
    heads = v.shape[0] // (2 * HEAD_CH)
    return v.reshape(2, heads, HEAD_CH, -1).swapaxes(0, 1).reshape(v.shape[0], -1)


def local(
    tokens, w_in, w_forget, b_forget, rotation, w_outgate, gn_gain, w_out, rms_gain,
    w_gate, w_up, w_down, cotangent, buckets, lengths,
):
    width = tokens.shape[1]
    half = width // 2
    chan = lax.axis_index("chan")
    nch = b_forget.shape[0]
    piece = jnp.concatenate(
        [
            split_parts(w_in), w_forget.T, split_parts(w_outgate),
            jnp.zeros((WO0 - PAD0, width), BF),
            w_out.reshape(-1, 2, HEAD_CH, width).swapaxes(0, 1).reshape(-1, width),
            w_gate.T, w_up.T, w_down,
        ],
        axis=0,
    )
    gains = gn_gain.reshape(-1, 2, HEAD_CH).swapaxes(0, 1).reshape(2, nch)
    params = jnp.concatenate(
        [
            b_forget[None], jnp.cos(rotation)[None], jnp.sin(rotation)[None], gains,
            jnp.zeros((3, nch), F32),
        ],
        axis=0,
    )
    params = lax.dynamic_update_slice(jnp.zeros((8, half), F32), params, (0, chan * nch))
    w_all = lax.all_gather(piece, "chan", axis=0, tiled=False)
    g, grad_tokens, block_out = main_call(
        w_all, tokens, cotangent, params, rms_gain[None], buckets, lengths
    )
    g = lax.psum_scatter(g, "chan", scatter_dimension=0, tiled=False)
    g = lax.psum(g, "batch").astype(F32)
    grad_w_in = join_parts(g[:192]).T
    grad_w_forget = g[192:288].T
    grad_w_outgate = join_parts(g[288:480]).T
    grad_w_out = join_parts(g[WO0:WG0])
    hw = (WD0 - WG0) // 2
    grad_w_gate = g[WG0 : WG0 + hw].T
    grad_w_up = g[WG0 + hw : WD0].T
    grad_w_down = g[WD0:PIECE]
    own = lax.dynamic_slice(g[PAD0 : PAD0 + 2].reshape(4, half), (0, chan * nch), (4, nch))
    grad_b, grad_rot = own[0], own[1]
    grad_gn = join_parts(own[2:4].reshape(2 * nch, 1))[:, 0]
    grad_rms = lax.dynamic_slice(g[PAD0 + 2], (chan * 2 * nch,), (2 * nch,))
    return (
        block_out, grad_tokens, grad_w_in, grad_w_forget, grad_b, grad_rot, grad_w_outgate,
        grad_gn, grad_w_out, grad_rms, grad_w_gate, grad_w_up, grad_w_down,
    )


def solution(mesh):
    both = P(("batch", "chan"), None)
    cols, rows, vec = P(None, "chan"), P("chan", None), P("chan")
    return jax.shard_map(
        local,
        mesh=mesh,
        in_specs=(
            both, cols, cols, vec, vec, cols, vec, rows, P(), cols, cols, rows, both,
            P("batch"), P("batch", None),
        ),
        out_specs=(
            both, both, cols, cols, vec, vec, cols, vec, rows, vec, cols, cols, rows,
        ),
        check_vma=False,
    )
```

time: 1960 us -> 614 us (0.31); the launches traced: 1930 us -> 613 us
  local copies, waits for them, and re-layouts: 663 us -> 33.7 us
  waiting for transfers between devices: 918 us -> 463 us
  other arithmetic: 217 us -> 2.24 us
  Pallas kernels: 0 us -> 99.6 us
  matrix products: 92 us -> 0 us
  blocking collectives: 23.5 us -> 0 us
    pad x118 -> x0, local copies, waits for them, and re-layouts: 270 us -> none  [recurrence(): lax.associative_scan(complex_combine, (prod_real, prod_imag, state_real,...]
    all_gather x4 -> x1, waiting for transfers between devices: 440 us -> 200 us  [local(): w_all = lax.all_gather(piece, 'chan', axis=0, tiled=False)]
    reduce_scatter x4 -> x1, waiting for transfers between devices: 378 us -> 192 us  [local(): g = lax.psum_scatter(g, 'chan', scatter_dimension=0, tiled=False)]
    slice x120 -> x5, local copies, waits for them, and re-layouts: 146 us -> 1.95 us  [the longest x1 1.09 us: local(): grad_w_down = g[WD0:PIECE]]
    unnamed x815 -> x33, local copies, waits for them, and re-layouts: 125 us -> 18.7 us
    pallas_call x0 -> x1, Pallas kernels: none -> 99.6 us  [main_call(): pl.pallas_call(main_kernel, out_shape=[jax.ShapeDtypeStruct(w_all.shape,...]
    dot_general x15 -> x0, matrix products: 92 us -> none  [the longest x10 57.3 us: contract(): lax.dot_general(left, right, (((left_dim,), (right_dim,)), ((), ())), pre...]
    add_any x46 -> x0, other arithmetic: 71.6 us -> none  [the longest x15 25.1 us: complex_combine(): latter[1] * former[3]]
  transfers between devices with their start and end apart: 9 -> 3, of which waited for: 8 -> 3; matrix products, arithmetic and copies ran while one was open for 26% -> 0% of each run, Pallas kernels for 0% -> 0%
where the time goes in v1:
time: 614 us; the launch traced here: 613 us
  waiting for transfers between devices  463 us (75%)
  Pallas kernels  99.6 us (16%)
  local copies, waits for them, and re-layouts  33.7 us (5%)
  between operations  14.6 us (2%)
    all_gather x1, waiting for transfers between devices, local(): w_all = lax.all_gather(piece, 'chan', axis=0, tiled=False)  200 us
    reduce_scatter x1, waiting for transfers between devices, local(): g = lax.psum_scatter(g, 'chan', scatter_dimension=0, tiled=False)  192 us
    pallas_call x1, Pallas kernels, main_call(): pl.pallas_call(main_kernel, out_shape=[jax.ShapeDtypeStruct(w_all.shape,...  99.6 us
    psum x1, waiting for transfers between devices, local(): g = lax.psum(g, 'batch').astype(F32)  71.6 us
    unnamed x33, local copies, waits for them, and re-layouts  18.7 us
  transfers between devices with their start and end apart: 3, of which 3 were waited for; matrix products, arithmetic and copies ran while one was open for 0% of the time, Pallas kernels for 0%

profile of v1, /device:TPU:0, one launch (start us, length us, event | category | flops | bytes accessed | tf_op | source)
XLA Modules:
  0.0 613.4 jit_solution(8169261022253847647)
XLA Ops:
  7.2 0.0 copy-start.3
  7.2 0.0 all-gather.3.cloned.1.call-start
  7.2 1.7 copy.38
  9.0 1.7 copy.39
  10.7 1.7 copy.40
  12.4 2.1 copy.41
  14.5 0.0 copy-done.3
  14.5 0.3 copy.42
  14.7 0.0 copy-start.4
  14.8 1.0 constant_dynamic-update-slice_fusion.3
  15.8 0.9 bitcast_dynamic-update-slice_fusion.2
  16.7 1.0 constant_dynamic-update-slice_fusion.2
  17.7 1.0 constant_dynamic-update-slice_fusion.1
  18.7 1.1 bitcast_dynamic-update-slice_fusion.1
  19.8 0.0 copy-start.7
  19.8 0.0 copy-start.6
  19.9 0.0 copy-start.9
  19.9 0.0 copy-start.8
  19.9 0.0 copy-done.4
  20.0 0.0 copy-start.1
  20.0 1.6 copy-done.1
  21.6 0.0 all-gather.3.cloned.1.call-update
  21.6 0.0 reduce-scatter.2.cloned.1.call-start
  22.3 0.0 copy-done.7
  22.3 0.1 reshape.78
  22.4 0.1 reshape.79
  22.5 0.0 copy-done.6
  22.5 0.6 broadcast_in_dim.27.rms_ref
  23.1 0.0 copy-done.9
  23.1 0.0 copy-done.8
  23.1 0.3 dynamic_update_slice.3.par_ref
  23.4 0.0 copy-start.5
  23.4 199.9 %all-gather.3.cloned.1.call-done = bf16[7424,768]{1,0:T(8,128)(2,1)} async-done(((bf16[1856,768]{1,0:T(8,128)(2,1)}), bf16[7424,768]{1,0:T(8,128)(2,1)}) %all-gather.3.cloned.1.call-update) | async-done | bytes 11403280 | tf_op jit(solution)/shard_map/all_gather | solution.py:535
  223.4 0.0 copy-done.5
  223.4 99.6 %block.1 = (bf16[4,1856,768]{2,1,0:T(8,128)(2,1)}, f32[1024,768]{1,0:T(8,128)}, bf16[1024,768]{1,0:T(8,128)(2,1)}) custom-call(bf16[4,1856,768]{2,1,0:T(8,128)(2,1)} %bitcast.77, bf16[1024,768]{1,0:T(8,128)(2,1)} %tok_hbm.1, bf16[1024,768]{1,0:T(8,128)(2,1)} %cot_hbm.1, f32[8,384]{1,0:T(8,128)} %copy-done.5, f32[1,768]{1,0:T(1,128)} %broadcast_in_dim.27.rms_ref, ...), custom_call_target="tpu_custom_call" | custom-call | flops 33999998976 | bytes 30000000 | tf_op jit(solution)/shard_map/block/pallas_call | solution.py:463
  323.0 0.0 reduce-scatter.2.cloned.1.call-update
  323.0 0.0 all-reduce.2.cloned.1.call-start
  323.1 191.5 %reduce-scatter.2.cloned.1.call-done = bf16[1,1856,768]{2,1,0:T(8,128)(2,1)} async-done(((bf16[4,1856,768]{2,1,0:T(8,128)(2,1)}), bf16[1,1856,768]{2,1,0:T(8,128)(2,1)}) %reduce-scatter.2.cloned.1.call-update) | async-done | bytes 2850832 | tf_op jit(solution)/shard_map/reduce_scatter | solution.py:539
  514.6 0.0 all-reduce.2.cloned.1.call-update
  514.6 71.6 %all-reduce.2.cloned.1.call-done = bf16[1856,768]{1,0:T(8,128)(2,1)} async-done(((bf16[1856,768]{1,0:T(8,128)(2,1)}), bf16[1856,768]{1,0:T(8,128)(2,1)}) %all-reduce.2.cloned.1.call-update) | async-done | bytes 2850832 | tf_op jit(solution)/shard_map/psum | solution.py:540
  586.2 0.7 slice.50
  586.9 0.1 constant_dynamic-slice_fusion.1
  587.0 0.5 slice_bitcast_fusion.3
  587.5 2.2 convert_element_type.3
  589.7 0.0 copy-start
  589.7 0.7 slice_bitcast_fusion.2
  590.5 1.6 slice_bitcast_fusion
  592.0 0.1 reshape_reshape.3
  592.1 0.6 squeeze_reshape.3
  592.8 0.0 copy-done
  592.8 0.1 fusion
  592.9 0.9 copy.47
  593.8 0.9 copy.45
  594.6 0.9 copy.44
  595.5 2.7 copy.49
  598.1 2.7 copy.48
  600.8 0.0 copy-start.2
  600.8 0.6 constant_dynamic-slice_fusion
  601.4 1.1 slice.56
  602.5 2.7 copy.62
  605.2 0.0 copy-done.2
  605.2 1.7 copy.63
  (12 shorter events, 0.2 us)
Async XLA Ops:
  7.2 7.3 %copy-start.3 = (bf16[768,384]{1,0:T(8,128)(2,1)S(1)}, bf16[768,384]{1,0:T(8,128)(2,1)}, u32[]{:S(2)}) copy-start(bf16[768,384]{1,0:T(8,128)(2,1)} %param.25) | copy-start | bytes 1769476
  7.2 216.2 %all-gather.3.cloned.1.call-start = ((), (), s32[]{:S(2)}) async-start(), calls=%async_computation.3 | async-start | bytes 14254080 | tf_op jit(solution)/shard_map/all_gather | solution.py:535
  14.7 5.2 copy-start.4
  19.8 2.5 copy-start.7
  19.8 2.6 copy-start.6
  19.9 3.2 copy-start.9
  19.9 3.2 copy-start.8
  20.0 1.6 copy-start.1
  21.6 493.0 %reduce-scatter.2.cloned.1.call-start = ((), (), s32[]{:S(2)}) async-start(), calls=%async_computation.1 | async-start | bytes 14254080 | tf_op jit(solution)/shard_map/reduce_scatter | solution.py:539
  23.4 200.0 %copy-start.5 = (f32[8,384]{1,0:T(8,128)}, f32[8,384]{1,0:T(8,128)S(1)}, u32[]{:S(2)}) copy-start(f32[8,384]{1,0:T(8,128)S(1)} %dynamic_update_slice.3.par_ref) | copy-start | bytes 36868
  323.0 263.1 %all-reduce.2.cloned.1.call-start = ((), (), s32[]{:S(2)}) async-start(), calls=%async_computation.2 | async-start | bytes 5701632 | tf_op jit(solution)/shard_map/psum | solution.py:540
  589.7 3.0 copy-start
  600.8 4.4 copy-start.2
Sparse Core Ops, SparseCore 0:
  21.7 201.6 all-gather.2
  323.1 191.3 reduce-scatter.1
  518.2 67.8 all-reduce.1

commit v2 on v1

--- a/solution.py
+++ b/solution.py
@@ -12,9 +12,9 @@
 F32 = jnp.float32
 HEAD_CH = 32
 SEGS = 16
-TM = 256
-MT0, WO0, WG0, WD0, PIECE = 0, 512, 704, 1472, 1856
-PAD0 = 480
+TM = SEGS * SEGS
+PAD0, MA0, WO0, WG0, WD0, PIECE = 288, 320, 512, 704, 1472, 1856
+SECTION = (0, 96, 192, 320, 416)
 
 
 def dot(left, right, left_dim, right_dim):
@@ -28,7 +28,20 @@
 
 
 def sigmoid(v):
-    return 1.0 / (1.0 + jnp.exp(-v))
+    return 0.5 * jnp.tanh(0.5 * v) + 0.5
+
+
+def tiles(count, body, steps=None):
+    @pl.loop(0, count)
+    def _(i):
+        for at, calls in (steps or {}).items():
+
+            @pl.when(i == at)
+            def _(calls=calls):
+                for call in calls:
+                    call()
+
+        body(i)
 
 
 def get(ref, rows, first, count):
@@ -45,14 +58,18 @@
 
 
 def main_kernel(
-    w_hbm, tok_hbm, cot_hbm, par_ref, rms_ref, bucket_ref, len_ref,
+    n_batch, n_chan,
+    win_hbm, wf_hbm, wg_hbm, wout_hbm, wgate_hbm, wup_hbm, wdown_hbm, tok_hbm, cot_hbm,
+    bias_ref, rot_ref, gn_ref, rms_ref, bucket_ref, len_ref,
     g_hbm, gtok_hbm, out_hbm,
     w, tok, sd, pv, om, pg, ws, xh, rstd, res, fin, mix, out, dff, hid, dgu, dm, dp,
-    ones, parx, carx, carb, seg, sgrad, seg_prod,
+    ones, swap, parx, carx, carb, seg, sgrad, seg_prod,
+    rb0, rb1, rb2, zbf, zba, zbb, mixf, extra,
+    par_own,
     load_sem, store_sem, par_send, par_recv, car_send, car_recv, cab_send, cab_recv,
+    ag_send, ag_recv, rs_send, rs_recv, fin_send, fin_recv, ex_send, ex_recv,
 ):
-    n_chan, n_rows = 4, tok.shape[0]
-    width = tok.shape[1]
+    n_rows, width = tok.shape
     half = width // 2
     lt = half // 128
     n_tiles = n_rows // TM
@@ -60,41 +77,335 @@
     b = lax.axis_index("batch")
     c = lax.axis_index("chan")
     peers = [lax.rem(c + j, n_chan) for j in range(1, n_chan)]
-
-    loads = [
-        pltpu.make_async_copy(tok_hbm, tok, load_sem.at[0]),
-        pltpu.make_async_copy(w_hbm, w, load_sem.at[1]),
-        pltpu.make_async_copy(cot_hbm, sd, load_sem.at[2]),
-    ]
-    for load in loads:
-        load.start()
+    core = lax.rem(b, 2)
+    quarter = lax.rem(b // 2, 4)
+    x_bit, y_bit = lax.rem(quarter, 2), quarter // 2
+
+    def flip(bit):
+        here = b
+        for k in range(n_batch.bit_length()):
+            if bit >> k & 1:
+                here = here + (1 << k) - (2 << k) * lax.rem(b // (1 << k), 2)
+        return here
+
+    core_dev, x_dev, y_dev, diag_dev = ((flip(bit), c) for bit in (1, 2, 4, 6))
+    extra_devs = [(flip(1 << k), c) for k in range(3, n_batch.bit_length() - 1)]
+    mine = pl.ds(pl.multiple_of(core * half, 128), half)
+    theirs = pl.ds(pl.multiple_of((1 - core) * half, 128), half)
+
+    def span(start, size):
+        return pl.ds(pl.multiple_of(start, 16), size)
+
+    def remote(src, dst, send_sem, recv_sem, device):
+        return pltpu.make_async_remote_copy(
+            src, dst, send_sem, recv_sem, device_id=device, device_id_type=MESH
+        )
+
+    nch = bias_ref.shape[1]
+    heads = nch // HEAD_CH
+
+    def load(src, dst, k):
+        copy = pltpu.make_async_copy(src, dst, load_sem.at[k])
+        copy.start()
+        return copy
+
+    def load_heads(src, first, at):
+        return [
+            load(
+                src.at[HEAD_CH * (2 * hh + part) : HEAD_CH * (2 * hh + part + 1), :],
+                w.at[c, pl.ds(first + nch * part + HEAD_CH * hh, HEAD_CH), :],
+                at + 2 * hh + part,
+            )
+            for hh in range(heads)
+            for part in range(2)
+        ]
+
+    load_first = load_heads(win_hbm, 0, 6) + [load(wf_hbm, w.at[c, pl.ds(2 * nch, nch), :], 0)]
+    load_second = load_heads(wg_hbm, MA0, 6 + 2 * heads) + load_heads(wout_hbm, WO0, 6 + 4 * heads)
+    load_gate = load(wgate_hbm, hid.at[:width, :], 1)
+    load_up = load(wup_hbm, dgu.at[:width, : hid.shape[1]], 2)
+    load_down = load(wdown_hbm, w.at[c, WD0:PIECE, :], 3)
+    load_tok = load(tok_hbm, fin, 4)
+    load_cot = load(cot_hbm, dm.at[:n_rows, :], 5)
 
     barrier = pltpu.get_barrier_semaphore()
-    for peer in peers:
-        pl.semaphore_signal(barrier, inc=1, device_id=(b, peer), device_id_type=MESH)
-    pl.semaphore_wait(barrier, n_chan - 1)
+    talk = [core_dev, x_dev, y_dev, diag_dev] + extra_devs + [(b, peer) for peer in peers]
+    for device in talk:
+        pl.semaphore_signal(barrier, inc=1, device_id=device, device_id_type=MESH)
+
+    w[c, PAD0:MA0, :] = jnp.zeros((MA0 - PAD0, width), BF)
+    par_own[...] = jnp.zeros_like(par_own)
+    par_own[0:1, :nch] = bias_ref[...]
+    par_own[1:2, :nch] = jnp.cos(rot_ref[...])
+    par_own[2:3, :nch] = jnp.sin(rot_ref[...])
+    for hh in range(heads):
+        for part in range(2):
+            at = HEAD_CH * (2 * hh + part)
+            par_own[3 + part : 4 + part, HEAD_CH * hh : HEAD_CH * (hh + 1)] = gn_ref[
+                :, at : at + HEAD_CH
+            ]
+    parx[c] = pltpu.roll(par_own[...], c * nch, 1)
+    pl.semaphore_wait(barrier, len(talk))
 
     def exchange(ref, send_sem, recv_sem):
         copies = [
-            pltpu.make_async_remote_copy(
-                ref.at[c], ref.at[c], send_sem.at[j], recv_sem.at[j],
-                device_id=(b, peer), device_id_type=MESH,
-            )
+            remote(ref.at[c], ref.at[c], send_sem.at[j], recv_sem.at[j], (b, peer))
             for j, peer in enumerate(peers)
         ]
         return copies
 
-    parx[c] = par_ref[...]
+    class Gather:
+        def __init__(self, unit, j, first, count, turns):
+            self.first, self.count, self.turns = first, count, turns
+            src = lax.rem(c + j, n_chan)
+            peer = lax.rem(c + n_chan - j, n_chan)
+            send, recv = ag_send.at[unit], ag_recv.at[unit]
+
+            def copy(k, chan, rows, device):
+                ref = w.at[chan, rows, mine]
+                return remote(ref, ref, send.at[k], recv.at[k], device)
+
+            from_x = y_bit * 2 + 1 - x_bit
+            from_y = (1 - y_bit) * 2 + x_bit
+            own = self.rows(quarter)
+            self.z = copy(0, c, own, (b, peer))
+            self.p1 = [copy(1, src, own, x_dev), copy(2, src, own, y_dev)]
+            self.c1 = copy(3, src, own, core_dev)
+            if turns:
+                cut = count // 4 // 32 * 16
+                rest = count // 4 - cut
+                self.p2 = [
+                    copy(4, src, self.rows(from_x, 0, cut), y_dev),
+                    copy(5, src, self.rows(from_y, cut, rest), x_dev),
+                ]
+            else:
+                self.p2 = [copy(4, src, own, diag_dev)]
+            self.c2 = [copy(6, src, self.rows(from_x), core_dev),
+                       copy(7, src, self.rows(from_y), core_dev)]
+            self.c3 = copy(8, src, self.rows(3 - quarter), core_dev)
+
+        def rows(self, part, start=0, size=None):
+            size = self.count // 4 if size is None else size
+            return span(self.first + part * (self.count // 4) + start, size)
+
+        def along(self):
+            self.z.start()
+
+        def plane(self):
+            self.z.wait_recv()
+            for copy in self.p1 + [self.c1] + ([] if self.turns else self.p2):
+                copy.start()
+
+        def turn(self):
+            for copy in self.p1:
+                copy.wait_recv()
+            for copy in (self.p2 if self.turns else []) + self.c2:
+                copy.start()
+
+        def cross(self):
+            for copy in self.p2:
+                copy.wait_recv()
+            self.c3.start()
+
+        def ready(self):
+            for copy in [self.c1] + self.c2 + [self.c3]:
+                copy.wait_recv()
+
+        def along_free(self):
+            self.z.wait_send()
+
+        def free(self):
+            for copy in self.p1 + self.p2 + [self.c1] + self.c2 + [self.c3]:
+                copy.wait_send()
+
+    gather_a = [Gather(j - 1, j, 0, MA0, False) for j in range(1, n_chan)]
+    gather_b = [Gather(2 + j, j, MA0, WG0 - MA0, True) for j in range(1, n_chan)]
+    gather_f = [Gather(5 + j, j, WG0, PIECE - WG0, True) for j in range(1, n_chan)]
+
+    def in_w(chan, start, size, cols):
+        return w.at[chan, span(start, size), cols]
+
+    def in_dm(chan, start, size, cols):
+        return dm.at[span(chan * MA0 + start, size), cols]
+
+    class Reduce:
+        def __init__(self, chunk, distances, count, first, slots, ref):
+            self.first, self.count, self.ref = first, count, ref
+            send, recv = rs_send.at[chunk], rs_recv.at[chunk]
+            q = count // 4
+            cut = q // 32 * 16
+            rest = q - cut
+            bufs = [buf.at[chunk % 2] for buf in (rb0, rb1, rb2)]
+            used = [0, 0, 0]
+            k = 0
+
+            def place(level, size):
+                at = used[level]
+                used[level] += size
+                return bufs[level].at[at : at + size, :]
+
+            def rows(part, start, size):
+                return first + part * q + start, size
+
+            def copy(chan, rows, cols, dst, device):
+                nonlocal k
+                k += 1
+                return remote(ref(chan, *rows, cols), dst, send.at[k - 1], recv.at[k - 1], device)
+
+            self.s0, self.s1, self.s2, self.s3 = [], [], [], []
+            near_x, far_x = quarter, y_bit * 2 + 1 - x_bit
+            far_y = (1 - y_bit) * 2 + x_bit
+            for j in distances:
+                chan = lax.rem(c + j, n_chan)
+                whole = first, count
+                buf = place(0, count)
+                self.s0.append((chan, first, count, buf, copy(chan, whole, theirs, buf, core_dev)))
+                for part in range(2):
+                    buf = place(1, cut)
+                    self.s1.append((
+                        chan, first + (part * 2 + x_bit) * q, cut, buf,
+                        copy(chan, rows(part * 2 + 1 - x_bit, 0, cut), mine, buf, x_dev),
+                    ))
+                    buf = place(1, rest)
+                    self.s1.append((
+                        chan, first + (y_bit * 2 + part) * q + cut, rest, buf,
+                        copy(chan, rows((1 - y_bit) * 2 + part, cut, rest), mine, buf, y_dev),
+                    ))
+                buf = place(2, cut)
+                self.s2.append((
+                    chan, first + quarter * q, cut, buf,
+                    copy(chan, rows(far_y, 0, cut), mine, buf, y_dev),
+                ))
+                buf = place(2, rest)
+                self.s2.append((
+                    chan, first + quarter * q + cut, rest, buf,
+                    copy(chan, rows(far_x, cut, rest), mine, buf, x_dev),
+                ))
+                if j:
+                    self.s3.append(
+                        copy(chan, rows(quarter, 0, q), mine, slots.at[j - 1], (b, chan))
+                    )
+            self.sent = [item[-1] for item in self.s0 + self.s1 + self.s2] + self.s3
+
+        def add(self, items):
+            for chan, start, size, buf, copy in items:
+                copy.wait_recv()
+                for at in range(0, size, 96):
+                    n = min(96, size - at)
+                    here = self.ref(chan, start + at, n, mine)
+                    here[...] = (here[...].astype(F32) + buf[at : at + n, :].astype(F32)).astype(BF)
+
+        def to_core(self):
+            for item in self.s0:
+                item[-1].start()
+
+        def to_plane(self):
+            self.add(self.s0)
+            for item in self.s1:
+                item[-1].start()
+
+        def turn(self):
+            self.add(self.s1)
+            for item in self.s2:
+                item[-1].start()
+
+        def along(self):
+            self.add(self.s2)
+            for copy in self.s3:
+                copy.start()
+
+        def free(self):
+            for copy in self.sent:
+                copy.wait_send()
+
+    class Spread:
+        def __init__(self, chunk, ref, first, count, slots, recvs, dest, dest_first, ex_at):
+            self.ref, self.first, self.q = ref, first, count // 4
+            self.slots, self.recvs, self.dest = slots, recvs, dest
+            send, recv = fin_send.at[chunk], fin_recv.at[chunk]
+            self.at = span(dest_first + quarter * self.q, self.q)
+            ref = dest.at[self.at, mine]
+            self.copies = [
+                remote(ref, ref, send.at[k], recv.at[k], device)
+                for k, device in enumerate((x_dev, y_dev, diag_dev))
+            ]
+            ref_all = dest.at[dest_first : dest_first + count, mine]
+            self.last = remote(ref_all, ref_all, send.at[3], recv.at[3], core_dev)
+            self.extra = []
+            for k, device in enumerate(extra_devs):
+                buf = extra.at[k, ex_at : ex_at + self.q, :]
+                self.extra.append((buf, remote(
+                    ref, buf, ex_send.at[chunk, k], ex_recv.at[chunk, k], device
+                )))
+
+        def total(self):
+            for copy in self.recvs:
+                copy.wait_recv()
+            v = self.ref(c, self.first + quarter * self.q, self.q, mine)[...].astype(F32)
+            for j in range(n_chan - 1):
+                v = v + self.slots[j].astype(F32)
+            self.dest[self.at, mine] = v.astype(BF)
+            for buf, copy in self.extra:
+                copy.start()
+                copy.wait()
+                v = self.dest[self.at, mine].astype(F32) + buf[...].astype(F32)
+                self.dest[self.at, mine] = v.astype(BF)
+            for copy in self.copies:
+                copy.start()
+
+        def cross(self):
+            for copy in self.copies:
+                copy.wait_recv()
+            self.last.start()
+
+        def done(self):
+            self.last.wait_recv()
+            for copy in self.copies + [self.last]:
+                copy.wait_send()
+
+    reduce_f = [Reduce(j, [j], PIECE - WG0, WG0, zbf, in_w) for j in range(n_chan)]
+    reduce_a = Reduce(n_chan, range(n_chan), WG0 - MA0, MA0, zba, in_w)
+    reduce_b = Reduce(n_chan + 1, range(n_chan), MA0, 0, zbb, in_dm)
+    spread_f = Spread(
+        0, in_w, WG0, PIECE - WG0, zbf, [copy for r in reduce_f for copy in r.s3], dgu, 0, 0
+    )
+    spread_a = Spread(1, in_w, MA0, WG0 - MA0, zba, reduce_a.s3, mixf, MA0, (PIECE - WG0) // 4)
+    spread_b = Spread(2, in_dm, 0, MA0, zbb, reduce_b.s3, mixf, 0, (PIECE - MA0) // 4)
+
+    for copy in load_first:
+        copy.wait()
+    for g in gather_a:
+        g.along()
     par_copies = exchange(parx, par_send, par_recv)
     for copy in par_copies:
         copy.start()
+    for copy in load_second:
+        copy.wait()
+    for g in gather_b:
+        g.along()
+    hw = hid.shape[1]
+    load_gate.wait()
+    w[c, WG0 : WG0 + hw, :] = hid[:width, :].T
+    load_up.wait()
+    w[c, WG0 + hw : WD0, :] = dgu[:width, :hw].T
+    load_down.wait()
+    for g in gather_f:
+        g.along()
     lane_r = lax.broadcasted_iota(jnp.int32, (half, half), 0) // HEAD_CH
     lane_c = lax.broadcasted_iota(jnp.int32, (half, half), 1) // HEAD_CH
     ones[...] = jnp.where(lane_r == lane_c, 1.0 / (2 * HEAD_CH), 0.0).astype(BF)
     sgrad[...] = jnp.zeros_like(sgrad)
-
-    def head_mean(v):
+    row = lax.broadcasted_iota(jnp.int32, (TM, TM), 0)
+    col = lax.broadcasted_iota(jnp.int32, (TM, TM), 1)
+    swap[...] = jnp.where(row == lax.rem(col, SEGS) * SEGS + col // SEGS, 1.0, 0.0).astype(BF)
+
+    def blocks(i):
+        return [span(seg_len * k + SEGS * i, SEGS) for k in range(SEGS)]
+
+    def head_mean(v, exact=False):
         high = v.astype(BF)
+        if not exact:
+            return dot(high, ones[...], 1, 0)
         low = (v - high.astype(F32)).astype(BF)
         return dot(high, ones[...], 1, 0) + dot(low, ones[...], 1, 0)
 
@@ -127,12 +438,9 @@
     seg_cos, seg_sin = power(seg_len)
     all_cos, all_sin = power(n_rows)
 
-    loads[0].wait()
-    loads[1].wait()
-
     def section(k):
         return jnp.concatenate(
-            [w[cc, 96 * k : 96 * k + 96, :] for cc in range(n_chan)], axis=0
+            [w[cc, SECTION[k] : SECTION[k] + 96, :] for cc in range(n_chan)], axis=0
         )
 
     def out_rows(k):
@@ -140,8 +448,33 @@
             [w[cc, WO0 + 96 * k : WO0 + 96 * k + 96, :] for cc in range(n_chan)], axis=0
         )
 
-    @pl.loop(0, n_tiles)
-    def _(i):
+    def order_tokens(i):
+        part = jnp.concatenate([fin[at, :] for at in blocks(i)], axis=0)
+        tok[rows_of(i, TM), :] = dot(swap[...], part, 1, 0).astype(BF)
+
+    def order_seed(i):
+        part = jnp.concatenate([dm[at, :] for at in blocks(i)], axis=0).astype(F32)
+        k = lax.broadcasted_iota(jnp.int32, (TM, 1), 0)
+        place = k // SEGS * seg_len + lax.rem(k, SEGS) + SEGS * i
+        part = (part * jnp.where(place < live_rows, 1.0, 0.0)).astype(BF)
+        sd[rows_of(i, TM), :] = dot(swap[...], part, 1, 0).astype(BF)
+
+    load_tok.wait()
+    tiles(n_tiles, order_tokens)
+    for g in gather_a:
+        g.plane()
+    load_cot.wait()
+    tiles(n_tiles, order_seed)
+    for g in gather_b:
+        g.plane()
+    for g in gather_a:
+        g.turn()
+    for g in gather_a:
+        g.cross()
+    for g in gather_a:
+        g.ready()
+
+    def project(i):
         rows = rows_of(i, TM)
         x = tok[rows, :]
         for k in range(2):
@@ -150,8 +483,14 @@
             put(out, rows, k * lt, pre * sigmoid(pre))
         put(om, rows, 0, 1.0 / (1.0 + jnp.exp(dot(x, section(2), 1, 1) + bias)))
 
+    tiles(n_tiles, project, {
+        1: [g.turn for g in gather_b],
+        3: [g.cross for g in gather_b],
+    })
+    gather_f[0].plane()
+
     def strided(t):
-        return pl.ds(t, SEGS, stride=seg_len)
+        return span(t * SEGS, SEGS)
 
     def first(t, carry):
         sr, si, prod = carry
@@ -195,14 +534,16 @@
     car_copies = exchange(carx, car_send, car_recv)
     for copy in car_copies:
         copy.start()
-
-    @pl.loop(0, n_tiles)
-    def _(i):
+    for g in gather_b:
+        g.ready()
+
+    def project_gate(i):
         rows = rows_of(i, TM)
         x = tok[rows, :]
         for k in range(2):
             pg[rows, k * half : (k + 1) * half] = dot(x, section(3 + k), 1, 1)
 
+    tiles(n_tiles, project_gate, {1: [gather_f[1].plane], 2: [gather_f[0].turn]})
     for copy in car_copies:
         copy.wait()
     cr, ci = zrow, zrow
@@ -228,15 +569,14 @@
 
     lax.fori_loop(0, seg_len, second, (seg[2], seg[3]), unroll=4)
 
-    @pl.loop(0, n_tiles)
-    def _(i):
+    def mixer_out(i):
         rows = rows_of(i, TM)
         o = get(om, rows, 0, lt)
         f = 1.0 - o
         gr, gi = pg[rows, :half], pg[rows, half:]
         yr = gr * sigmoid(gr) * (f * get(ws, rows, 0, lt) + o * get(out, rows, 0, lt))
         yi = gi * sigmoid(gi) * (f * get(ws, rows, lt, lt) + o * get(out, rows, lt, lt))
-        mean = head_mean(yr + yi)
+        mean = head_mean(yr + yi, True)
         yr, yi = yr - mean, yi - mean
         inv = lax.rsqrt(head_mean(yr * yr + yi * yi) + 1e-5)
         yr, yi = yr * inv, yi * inv
@@ -255,23 +595,17 @@
         fin[rows, :] = (r * rinv * rms_gain).astype(BF)
         dff[rows, :] = jnp.zeros((TM, width), F32)
 
-    loads[2].wait()
-
-    @pl.loop(0, n_tiles)
-    def _(i):
-        rows = rows_of(i, TM)
-        place = lax.broadcasted_iota(jnp.int32, (TM, 1), 0) + i * TM
-        live = jnp.where(place < live_rows, 1.0, 0.0)
-        sd[rows, :] = (sd[rows, :].astype(F32) * live).astype(BF)
-
-    hw = hid.shape[1]
-
-    @pl.loop(0, n_chan)
-    def _(j):
+    tiles(n_tiles, mixer_out, {
+        0: [gather_f[0].cross],
+        1: [gather_f[1].turn, gather_f[2].plane],
+        2: [gather_f[0].ready, gather_f[1].cross],
+        3: [gather_f[2].turn],
+    })
+
+    for j in range(n_chan):
         cc = lax.rem(c + j, n_chan)
 
-        @pl.loop(0, n_tiles)
-        def _(i):
+        def feed(i, cc=cc):
             rows = rows_of(i, TM)
             gate_up = dot(fin[rows, :], w[cc, WG0:WD0, :], 1, 1)
             d_hid = dot(sd[rows, :], w[cc, WD0:PIECE, :], 1, 1)
@@ -287,16 +621,31 @@
             put(out, rows, 0, get(out, rows, 0, 2 * lt) + dot(h, w[cc, WD0:PIECE, :], 1, 0))
             dff[rows, :] += dot(dgu[rows, :], w[cc, WG0:WD0, :], 1, 0)
 
+        if j == 0:
+            tiles(n_tiles, feed, {0: [gather_f[2].cross], 1: [gather_f[1].ready]})
+            for g in gather_f:
+                g.along_free()
+        else:
+            before = reduce_f[j - 1]
+            older = [reduce_f[j - 2]] if j > 1 else []
+            if j == n_chan - 1:
+                gather_f[j - 1].ready()
+            tiles(n_tiles, feed, {1: [r.turn for r in older], 2: [before.to_plane]})
+            gather_f[j - 1].free()
         for k in range(2):
             w[cc, WG0 + hw * k : WG0 + hw * (k + 1), :] = dot(
-                dgu[:, hw * k : hw * (k + 1)], fin[...], 0, 0
+                dgu[:n_rows, hw * k : hw * (k + 1)], fin[...], 0, 0
             ).astype(BF)
         w[cc, WD0:PIECE, :] = dot(hid[...], sd[...], 0, 0).astype(BF)
-
-    @pl.loop(0, n_tiles)
-    def _(i):
+        if j > 1:
+            older[0].along()
+        reduce_f[j].to_core()
+
+    def mixer_back(i):
         rows = rows_of(i, TM)
-        fin[rows, :] = get(out, rows, 0, 2 * lt).astype(BF)
+        done = dot(swap[...], get(out, rows, 0, 2 * lt).astype(BF), 1, 0).astype(BF)
+        for k, at in enumerate(blocks(i)):
+            fin[at, :] = done[SEGS * k : SEGS * (k + 1), :]
         r = res[rows, :]
         rinv = lax.rsqrt(jnp.mean(r * r, axis=1, keepdims=True) + 1e-6)
         rhat = r * rinv
@@ -333,9 +682,31 @@
                 dy * state * (sig + act * (1.0 - sig))
             ).astype(BF)
             put(out, rows, k * lt, dy * act)
-
+        acc = dff[rows, :]
+        for k in range(3, 5):
+            acc += dot(dp[rows, k * half : (k + 1) * half], section(k), 1, 0)
+        dff[rows, :] = acc
+
+    tiles(n_tiles, mixer_back, {
+        0: [reduce_f[-2].turn],
+        1: [reduce_f[-1].to_plane],
+        3: [reduce_f[-2].along],
+    })
     out_copy = pltpu.make_async_copy(fin, out_hbm, store_sem.at[0])
     out_copy.start()
+
+    for g in gather_a + gather_b:
+        g.along_free()
+        g.free()
+    for k in range(4):
+        left = mix[:, k * half : (k + 1) * half] if k < 2 else dp[:, (k + 1) * half : (k + 2) * half]
+        grad = dot(left, dm[:n_rows, :] if k < 2 else tok[...], 0, 0).astype(BF)
+        to = WO0 + 96 * k if k < 2 else SECTION[k + 1]
+        for cc in range(n_chan):
+            w[cc, to : to + 96, :] = grad[96 * cc : 96 * cc + 96, :]
+        if k == 1:
+            reduce_f[-1].turn()
+    reduce_a.to_core()
 
     def first_back(k, carry):
         qr, qi = carry
@@ -369,10 +740,8 @@
     for copy in car_copies:
         copy.start()
 
-    for k in range(2):
-        grad = dot(mix[:, k * half : (k + 1) * half], dm[...], 0, 0).astype(BF)
-        for cc in range(n_chan):
-            w[cc, WO0 + 96 * k : WO0 + 96 * k + 96, :] = grad[96 * cc : 96 * cc + 96, :]
+    reduce_f[-1].along()
+    reduce_a.to_plane()
 
     for copy in car_copies:
         copy.wait()
@@ -396,9 +765,7 @@
         return f * (cos16 * lr + sin16 * li), f * (cos16 * li - sin16 * lr)
 
     lax.fori_loop(0, seg_len, second_back, (seg[2], seg[3]), unroll=4)
-
-    @pl.loop(0, n_tiles)
-    def _(i):
+    def project_back(i):
         rows = rows_of(i, TM)
         o = get(om, rows, 0, lt)
         f = 1.0 - o
@@ -421,37 +788,173 @@
                 - get(out, rows, 0, lt) * get(ws, rows, lt, lt)
             )
         )
-        acc = dff[rows, :]
-        for k in range(5):
-            acc += dot(dp[rows, k * half : (k + 1) * half], section(k), 1, 0)
-        dff[rows, :] = acc
-
-    gtok_copy = pltpu.make_async_copy(dff, gtok_hbm, store_sem.at[1])
-    gtok_copy.start()
-
+
+    tiles(n_tiles, project_back)
     small = jnp.concatenate(
         [jnp.sum(sgrad[k], axis=0, keepdims=True) for k in range(3)]
-        + [jnp.zeros((13, width), F32)],
+        + [jnp.zeros((29, width), F32)],
         axis=0,
     ).astype(BF)
     for cc in range(n_chan):
-        w[cc, PAD0 : PAD0 + 16, :] = small
-        w[cc, PAD0 + 16 : WO0, :] = jnp.zeros((16, width), BF)
-    for k in range(5):
+        dm[MA0 * cc + PAD0 : MA0 * (cc + 1), :] = small
+    for k in range(3):
         grad = dot(dp[:, k * half : (k + 1) * half], tok[...], 0, 0).astype(BF)
         for cc in range(n_chan):
-            w[cc, 96 * k : 96 * k + 96, :] = grad[96 * cc : 96 * cc + 96, :]
-
-    g_copy = pltpu.make_async_copy(w, g_hbm, store_sem.at[2])
-    g_copy.start()
-    for copy in (out_copy, gtok_copy, g_copy):
+            at = MA0 * cc + 96 * k
+            dm[at : at + 96, :] = grad[96 * cc : 96 * cc + 96, :]
+    reduce_b.to_core()
+    def d_tokens(i):
+        rows = rows_of(i, TM)
+        acc = dff[rows, :]
+        for k in range(3):
+            acc += dot(dp[rows, k * half : (k + 1) * half], section(k), 1, 0)
+        high = acc.astype(BF)
+        low = (acc - high.astype(F32)).astype(BF)
+        done = dot(swap[...], high, 1, 0) + dot(swap[...], low, 1, 0)
+        for k, at in enumerate(blocks(i)):
+            res[at, :] = done[SEGS * k : SEGS * (k + 1), :]
+
+    tiles(n_tiles, d_tokens, {
+        0: [spread_f.total, reduce_a.turn],
+        2: [reduce_b.to_plane],
+        3: [spread_f.cross],
+    })
+    gtok_copy = pltpu.make_async_copy(res, gtok_hbm, store_sem.at[1])
+    gtok_copy.start()
+    reduce_a.along()
+    reduce_b.turn()
+    spread_f.done()
+    g_copies = [pltpu.make_async_copy(dgu, g_hbm.at[WG0:PIECE, :], store_sem.at[2])]
+    g_copies[0].start()
+    spread_a.total()
+    reduce_b.along()
+    spread_a.cross()
+    spread_b.total()
+    spread_a.done()
+    spread_b.cross()
+    spread_b.done()
+    g_copies.append(pltpu.make_async_copy(mixf, g_hbm.at[:WG0, :], store_sem.at[3]))
+    g_copies[1].start()
+    for r in reduce_f + [reduce_a, reduce_b]:
+        r.free()
+    for copy in [out_copy, gtok_copy] + g_copies:
         copy.wait()
 
 
-def main_call(w_all, tokens, cotangent, params, rms, bucket, lengths):
+def post_kernel(
+    g_hbm, gtok_hbm, out_hbm,
+    win_ref, wf_ref, bf_ref, rot_ref, wg_ref, gn_ref, wout_ref, rms_ref, gate_ref, up_ref,
+    down_ref, gtok_ref, out_ref,
+    g, t_in, t_f, t_g, t_out, t_gate, t_up, t_down, t_gtok, t_block, rows8, load_sem, store_sem,
+):
+    nch = bf_ref.shape[1]
+    heads = nch // HEAD_CH
+    hw = (WD0 - WG0) // 2
+    half = g.shape[1] // 2
+    c = lax.axis_index("chan")
+    cuts = (0, MA0, WG0, WG0 + hw, WD0, PIECE)
+    loads = []
+    for k in range(5):
+        rows = pl.ds(cuts[k], cuts[k + 1] - cuts[k])
+        loads.append(pltpu.make_async_copy(g_hbm.at[rows, :], g.at[rows, :], load_sem.at[k]))
+        loads[-1].start()
+    stage = [
+        pltpu.make_async_copy(gtok_hbm, t_gtok, load_sem.at[5]),
+        pltpu.make_async_copy(out_hbm, t_block, load_sem.at[6]),
+    ]
+    for copy in stage:
+        copy.start()
+    stores = []
+
+    def store(src, dst):
+        copy = pltpu.make_async_copy(src, dst, store_sem.at[len(stores)])
+        copy.start()
+        stores.append(copy)
+
+    def joined(first):
+        return jnp.concatenate(
+            [
+                g[first + nch * part + HEAD_CH * hh : first + nch * part + HEAD_CH * (hh + 1), :]
+                for hh in range(heads)
+                for part in range(2)
+            ],
+            axis=0,
+        )
+
+    loads[0].wait()
+    t_in[...] = joined(0).astype(F32)
+    store(t_in, win_ref)
+    t_f[...] = g[2 * nch : 3 * nch, :].astype(F32)
+    store(t_f, wf_ref)
+    small = g[PAD0 : PAD0 + 16, :].astype(F32)
+    turn = lax.rem(4 - c, 4) * nch
+    rows8[0:8, :half] = pltpu.roll(small[0:8, :half], turn, 1)
+    rows8[0:8, half:] = pltpu.roll(small[0:8, half:], turn, 1)
+    bf_ref[...] = rows8[0:1, :nch]
+    rot_ref[...] = rows8[0:1, half : half + nch]
+    for hh in range(heads):
+        for part in range(2):
+            at = half * part + HEAD_CH * hh
+            to = HEAD_CH * (2 * hh + part)
+            gn_ref[:, to : to + HEAD_CH] = rows8[1:2, at : at + HEAD_CH]
+    rows8[8:16, :] = pltpu.roll(small[0:8, :], 2 * turn, 1)
+    rms_ref[...] = rows8[10:11, : 2 * nch]
+    loads[1].wait()
+    t_g[...] = joined(MA0).astype(F32)
+    store(t_g, wg_ref)
+    t_out[...] = joined(WO0).astype(F32)
+    store(t_out, wout_ref)
+    loads[2].wait()
+    t_gate[...] = g[WG0 : WG0 + hw, :].T.astype(F32)
+    store(t_gate, gate_ref)
+    loads[3].wait()
+    t_up[...] = g[WG0 + hw : WD0, :].T.astype(F32)
+    store(t_up, up_ref)
+    loads[4].wait()
+    t_down[...] = g[WD0:PIECE, :].astype(F32)
+    store(t_down, down_ref)
+    for copy, src, dst in zip(stage, (t_gtok, t_block), (gtok_ref, out_ref), strict=True):
+        copy.wait()
+        store(src, dst)
+    for copy in stores:
+        copy.wait()
+
+
+def post_call(g, grad_tokens, block_out, nch):
+    width = g.shape[1]
+    hw = (WD0 - WG0) // 2
+    any_spec = pl.BlockSpec(memory_space=pl.ANY)
+    vmem = pl.BlockSpec(memory_space=pltpu.VMEM)
+    big = [(2 * nch, width), (nch, width), (2 * nch, width), (2 * nch, width), (width, hw),
+           (width, hw), (hw, width)]
+    shapes = [big[0], big[1], (1, nch), (1, nch), big[2], (1, 2 * nch), big[3], (1, 2 * nch),
+              big[4], big[5], big[6], grad_tokens.shape]
+    return pl.pallas_call(
+        post_kernel,
+        out_shape=[jax.ShapeDtypeStruct(shape, F32) for shape in shapes]
+        + [jax.ShapeDtypeStruct(block_out.shape, BF)],
+        in_specs=[any_spec] * 3,
+        out_specs=[vmem if shape[0] == 1 else any_spec for shape in shapes] + [any_spec],
+        scratch_shapes=[pltpu.VMEM(g.shape, BF)]
+        + [pltpu.VMEM(shape, F32) for shape in big + [grad_tokens.shape]]
+        + [
+            pltpu.VMEM(block_out.shape, BF),
+            pltpu.VMEM((16, width), F32),
+            pltpu.SemaphoreType.DMA((7,)),
+            pltpu.SemaphoreType.DMA((9,)),
+        ],
+        compiler_params=pltpu.CompilerParams(vmem_limit_bytes=48 * 2**20),
+        name="place",
+    )(g, grad_tokens, block_out)
+
+
+def main_call(weights, tokens, cotangent, vectors, bucket, lengths):
     rows, width = tokens.shape
     half = width // 2
-    n_chan = w_all.shape[0]
+    nch = vectors[0].shape[1]
+    n_chan, n_batch = lax.axis_size("chan"), lax.axis_size("batch")
+    n_extra = max(1, n_batch.bit_length() - 4)
+    w_shape = (n_chan, PIECE, width)
     hw = (WD0 - WG0) // 2
     any_spec = pl.BlockSpec(memory_space=pl.ANY)
     vmem = pl.BlockSpec(memory_space=pltpu.VMEM)
@@ -461,31 +964,45 @@
     tiles32 = pltpu.VMEM((width // 128, rows, 128), F32)
     full16 = pltpu.VMEM((rows, width), BF)
     return pl.pallas_call(
-        main_kernel,
+        functools.partial(main_kernel, n_batch, n_chan),
         out_shape=[
-            jax.ShapeDtypeStruct(w_all.shape, BF),
+            jax.ShapeDtypeStruct((PIECE, width), BF),
             jax.ShapeDtypeStruct((rows, width), F32),
             jax.ShapeDtypeStruct((rows, width), BF),
         ],
-        in_specs=[any_spec, any_spec, any_spec, vmem, vmem, smem, smem],
+        in_specs=[any_spec] * 9 + [vmem] * 4 + [smem, smem],
         out_specs=[any_spec] * 3,
         scratch_shapes=[
-            pltpu.VMEM(w_all.shape, BF),
+            pltpu.VMEM(w_shape, BF),
             full16, full16, full32, pltpu.VMEM((half // 128, rows, 128), F32), full32, tiles32,
             full32, half32, full32, full16, full16, tiles32, full32,
-            pltpu.VMEM((rows, hw), BF), pltpu.VMEM((rows, 2 * hw), BF),
-            full16, pltpu.VMEM((rows, 5 * half), BF),
+            pltpu.VMEM((rows, hw), BF), pltpu.VMEM((PIECE - WG0, 2 * hw), BF),
+            pltpu.VMEM((max(rows, n_chan * MA0), width), BF), pltpu.VMEM((rows, 5 * half), BF),
             pltpu.VMEM((half, half), BF),
+            pltpu.VMEM((TM, TM), BF),
             pltpu.VMEM((n_chan, 8, half), F32),
             pltpu.VMEM((n_chan, 8, half), F32),
             pltpu.VMEM((n_chan, 8, half), F32),
             pltpu.VMEM((4, SEGS, half), F32),
             pltpu.VMEM((3, 8, width), F32),
             pltpu.VMEM((SEGS, half), F32),
-            pltpu.SemaphoreType.DMA((3,)),
-            pltpu.SemaphoreType.DMA((3,)),
+            pltpu.VMEM((2, n_chan * (WG0 - MA0), half), BF),
+            pltpu.VMEM((2, n_chan * (WG0 - MA0) // 2, half), BF),
+            pltpu.VMEM((2, n_chan * (WG0 - MA0) // 4, half), BF),
+            pltpu.VMEM((n_chan - 1, (PIECE - WG0) // 4, half), BF),
+            pltpu.VMEM((n_chan - 1, (WG0 - MA0) // 4, half), BF),
+            pltpu.VMEM((n_chan - 1, MA0 // 4, half), BF),
+            pltpu.VMEM((WG0, width), BF),
+            pltpu.VMEM((n_extra, PIECE // 4, half) if n_batch > 8 else (1, 16, 128), BF),
+            pltpu.VMEM((8, half), F32),
+            pltpu.SemaphoreType.DMA((6 + 6 * nch // HEAD_CH,)),
+            pltpu.SemaphoreType.DMA((4,)),
         ]
-        + [pltpu.SemaphoreType.DMA((n_chan - 1,))] * 6,
+        + [pltpu.SemaphoreType.DMA((n_chan - 1,))] * 6
+        + [pltpu.SemaphoreType.DMA((3 * (n_chan - 1), 9))] * 2
+        + [pltpu.SemaphoreType.DMA((n_chan + 2, 8 * n_chan))] * 2
+        + [pltpu.SemaphoreType.DMA((3, 4))] * 2
+        + [pltpu.SemaphoreType.DMA((3, n_extra))] * 2,
         compiler_params=pltpu.CompilerParams(
             collective_id=0, has_side_effects=True, vmem_limit_bytes=60 * 2**20
         ),
@@ -493,66 +1010,24 @@
             flops=34 * 10**9, bytes_accessed=3 * 10**7, transcendentals=0
         ),
         name="block",
-    )(w_all, tokens, cotangent, params, rms, bucket, lengths)
-
-
-def split_parts(v):
-    heads = v.shape[1] // (2 * HEAD_CH)
-    return v.T.reshape(heads, 2, HEAD_CH, -1).swapaxes(0, 1).reshape(v.shape[1], -1)
-
-
-def join_parts(v):
-    heads = v.shape[0] // (2 * HEAD_CH)
-    return v.reshape(2, heads, HEAD_CH, -1).swapaxes(0, 1).reshape(v.shape[0], -1)
+    )(*weights, tokens, cotangent, *vectors, bucket, lengths)
 
 
 def local(
     tokens, w_in, w_forget, b_forget, rotation, w_outgate, gn_gain, w_out, rms_gain,
     w_gate, w_up, w_down, cotangent, buckets, lengths,
 ):
-    width = tokens.shape[1]
-    half = width // 2
-    chan = lax.axis_index("chan")
-    nch = b_forget.shape[0]
-    piece = jnp.concatenate(
-        [
-            split_parts(w_in), w_forget.T, split_parts(w_outgate),
-            jnp.zeros((WO0 - PAD0, width), BF),
-            w_out.reshape(-1, 2, HEAD_CH, width).swapaxes(0, 1).reshape(-1, width),
-            w_gate.T, w_up.T, w_down,
-        ],
-        axis=0,
+    g, grad_tokens, block_out = main_call(
+        (w_in.T, w_forget.T, w_outgate.T, w_out, w_gate, w_up, w_down), tokens, cotangent,
+        (b_forget[None], rotation[None], gn_gain[None], rms_gain[None]), buckets, lengths,
     )
-    gains = gn_gain.reshape(-1, 2, HEAD_CH).swapaxes(0, 1).reshape(2, nch)
-    params = jnp.concatenate(
-        [
-            b_forget[None], jnp.cos(rotation)[None], jnp.sin(rotation)[None], gains,
-            jnp.zeros((3, nch), F32),
-        ],
-        axis=0,
-    )
-    params = lax.dynamic_update_slice(jnp.zeros((8, half), F32), params, (0, chan * nch))
-    w_all = lax.all_gather(piece, "chan", axis=0, tiled=False)
-    g, grad_tokens, block_out = main_call(
-        w_all, tokens, cotangent, params, rms_gain[None], buckets, lengths
-    )
-    g = lax.psum_scatter(g, "chan", scatter_dimension=0, tiled=False)
-    g = lax.psum(g, "batch").astype(F32)
-    grad_w_in = join_parts(g[:192]).T
-    grad_w_forget = g[192:288].T
-    grad_w_outgate = join_parts(g[288:480]).T
-    grad_w_out = join_parts(g[WO0:WG0])
-    hw = (WD0 - WG0) // 2
-    grad_w_gate = g[WG0 : WG0 + hw].T
-    grad_w_up = g[WG0 + hw : WD0].T
-    grad_w_down = g[WD0:PIECE]
-    own = lax.dynamic_slice(g[PAD0 : PAD0 + 2].reshape(4, half), (0, chan * nch), (4, nch))
-    grad_b, grad_rot = own[0], own[1]
-    grad_gn = join_parts(own[2:4].reshape(2 * nch, 1))[:, 0]
-    grad_rms = lax.dynamic_slice(g[PAD0 + 2], (chan * 2 * nch,), (2 * nch,))
+    (
+        grad_w_in, grad_w_forget, grad_b, grad_rot, grad_w_outgate, grad_gn, grad_w_out, grad_rms,
+        grad_w_gate, grad_w_up, grad_w_down, grad_tokens, block_out,
+    ) = post_call(g, grad_tokens, block_out, b_forget.shape[0])
     return (
-        block_out, grad_tokens, grad_w_in, grad_w_forget, grad_b, grad_rot, grad_w_outgate,
-        grad_gn, grad_w_out, grad_rms, grad_w_gate, grad_w_up, grad_w_down,
+        block_out, grad_tokens, grad_w_in.T, grad_w_forget.T, grad_b[0], grad_rot[0],
+        grad_w_outgate.T, grad_gn[0], grad_w_out, grad_rms[0], grad_w_gate, grad_w_up, grad_w_down,
     )
 
 

time: 614 us -> 183 us (0.30)
  waiting for transfers between devices: 463 us -> 0 us
  Pallas kernels: 99.6 us -> 177 us
  local copies, waits for them, and re-layouts: 33.7 us -> 4.47 us
  between operations: 14.6 us -> 1.49 us
    all_gather x1 -> x0, waiting for transfers between devices: 200 us -> none  [local(): w_all = lax.all_gather(piece, 'chan', axis=0, tiled=False)]
    reduce_scatter x1 -> x0, waiting for transfers between devices: 192 us -> none  [local(): g = lax.psum_scatter(g, 'chan', scatter_dimension=0, tiled=False)]
    pallas_call x1 -> x2, Pallas kernels: 99.6 us -> 177 us  [the longest x1 169 us: main_call(): pl.pallas_call(functools.partial(main_kernel, n_batch, n_chan), out_shape...]
    psum x1 -> x0, waiting for transfers between devices: 71.6 us -> none  [local(): g = lax.psum(g, 'batch').astype(F32)]
    unnamed x33 -> x4, local copies, waits for them, and re-layouts: 18.7 us -> 3.21 us
  transfers between devices with their start and end apart: 3 -> 0, of which waited for: 3 -> 0; matrix products, arithmetic and copies ran while one was open for 0% -> 0% of each run, Pallas kernels for 0% -> 0%
where the time goes in v2:
time: 183 us
  Pallas kernels  177 us (97%)
  local copies, waits for them, and re-layouts  4.47 us (2%)
    pallas_call x1, Pallas kernels, main_call(): pl.pallas_call(functools.partial(main_kernel, n_batch, n_chan), out_shape...  169 us
    pallas_call x1, Pallas kernels, post_call(): pl.pallas_call(post_kernel, out_shape=[jax.ShapeDtypeStruct(shape, F32) f...  7.29 us

profile of v2, /device:TPU:0, one launch (start us, length us, event | category | flops | bytes accessed | tf_op | source)
XLA Modules:
  0.0 182.6 jit_solution(16948874929178477992)
XLA Ops:
  1.3 1.3 broadcast_in_dim.15.rms_ref
  2.6 169.4 %block.1 = (bf16[1856,768]{1,0:T(8,128)(2,1)}, f32[1024,768]{1,0:T(8,128)}, bf16[1024,768]{1,0:T(8,128)(2,1)}) custom-call(bf16[192,768]{1,0:T(8,128)(2,1)} %bitcast.15, bf16[96,768]{1,0:T(8,128)(2,1)} %bitcast.18, bf16[192,768]{1,0:T(8,128)(2,1)} %bitcast.16, bf16[192,768]{1,0:T(8,128)(2,1)} %wout_hbm.1, bf16[768,384]{1,0:T(8,128)(2,1)} %wgate_hbm.1, ...), custom_call_target="tpu_custom_call" | custom-call | flops 33999998976 | bytes 30000000 | tf_op jit(solution)/shard_map/block/pallas_call | solution.py:966
  172.0 0.0 copy-start
  172.0 1.8 copy-done
  173.8 0.0 copy-start.1
  173.8 1.4 copy-done.1
  175.2 7.3 %place.1 = (f32[192,768]{1,0:T(8,128)}, f32[96,768]{1,0:T(8,128)}, f32[1,96]{1,0:T(1,128)}, f32[1,96]{1,0:T(1,128)}, f32[192,768]{1,0:T(8,128)}, /*index=5*/f32[...) custom-call(bf16[1856,768]{1,0:T(8,128)(2,1)S(1)} %copy-done, ...), custom_call_target="tpu_custom_call" | custom-call | tf_op jit(solution)/shard_map/place/pallas_call | solution.py:932
Async XLA Ops:
  172.0 1.8 copy-start
  173.8 1.4 copy-start.1

commit v3 on v2

--- a/solution.py
+++ b/solution.py
@@ -64,7 +64,7 @@
     g_hbm, gtok_hbm, out_hbm,
     w, tok, sd, pv, om, pg, ws, xh, rstd, res, fin, mix, out, dff, hid, dgu, dm, dp,
     ones, swap, parx, carx, carb, seg, sgrad, seg_prod,
-    rb0, rb1, rb2, zbf, zba, zbb, mixf, extra,
+    rb0, rb1, rb2, mb0, mb1, mb2, zbf, zbm, mixf, extra,
     par_own,
     load_sem, store_sem, par_send, par_recv, car_send, car_recv, cab_send, cab_recv,
     ag_send, ag_recv, rs_send, rs_recv, fin_send, fin_recv, ex_send, ex_recv,
@@ -120,13 +120,19 @@
             for part in range(2)
         ]
 
-    load_first = load_heads(win_hbm, 0, 6) + [load(wf_hbm, w.at[c, pl.ds(2 * nch, nch), :], 0)]
-    load_second = load_heads(wg_hbm, MA0, 6 + 2 * heads) + load_heads(wout_hbm, WO0, 6 + 4 * heads)
+    load_first = load_heads(win_hbm, 0, 5 + n_chan) + [load(wf_hbm, w.at[c, pl.ds(2 * nch, nch), :], 0)]
+    load_second = (
+        load_heads(wg_hbm, MA0, 5 + n_chan + 2 * heads)
+        + load_heads(wout_hbm, WO0, 5 + n_chan + 4 * heads)
+    )
     load_gate = load(wgate_hbm, hid.at[:width, :], 1)
     load_up = load(wup_hbm, dgu.at[:width, : hid.shape[1]], 2)
     load_down = load(wdown_hbm, w.at[c, WD0:PIECE, :], 3)
     load_tok = load(tok_hbm, fin, 4)
-    load_cot = load(cot_hbm, dm.at[:n_rows, :], 5)
+    per = n_rows // n_chan
+    load_cot = [
+        load(cot_hbm.at[per * k : per * (k + 1), :], dm.at[k, :per, :], 5 + k) for k in range(n_chan)
+    ]
 
     barrier = pltpu.get_barrier_semaphore()
     talk = [core_dev, x_dev, y_dev, diag_dev] + extra_devs + [(b, peer) for peer in peers]
@@ -153,6 +159,25 @@
             for j, peer in enumerate(peers)
         ]
         return copies
+
+    def chain(ref, send_sem, recv_sem, up):
+        def each(out, call):
+            for k in range(n_chan):
+                above = c < k if out == up else c > k
+                copy = remote(
+                    ref.at[c] if out else ref.at[k], ref.at[c] if out else ref.at[k],
+                    send_sem.at[k], recv_sem.at[c] if out else recv_sem.at[k], (b, k),
+                )
+                pl.when(above)(functools.partial(call, copy))
+
+        def send():
+            each(True, lambda copy: copy.start())
+
+        def receive():
+            each(False, lambda copy: copy.wait_recv())
+            each(True, lambda copy: copy.wait_send())
+
+        return send, receive
 
     class Gather:
         def __init__(self, unit, j, first, count, turns):
@@ -218,82 +243,69 @@
             for copy in self.p1 + self.p2 + [self.c1] + self.c2 + [self.c3]:
                 copy.wait_send()
 
-    gather_a = [Gather(j - 1, j, 0, MA0, False) for j in range(1, n_chan)]
-    gather_b = [Gather(2 + j, j, MA0, WG0 - MA0, True) for j in range(1, n_chan)]
-    gather_f = [Gather(5 + j, j, WG0, PIECE - WG0, True) for j in range(1, n_chan)]
-
-    def in_w(chan, start, size, cols):
-        return w.at[chan, span(start, size), cols]
-
-    def in_dm(chan, start, size, cols):
-        return dm.at[span(chan * MA0 + start, size), cols]
+    ring = range(1, n_chan)
+    gather_a = [Gather(j - 1, j, 0, MA0, False) for j in ring]
+    gather_b = [Gather(2 + j, j, MA0, WO0 - MA0, True) for j in ring]
+    gather_o = [Gather(5 + j, j, WO0, WG0 - WO0, True) for j in ring]
+    gather_f = [Gather(8 + j, j, WG0, PIECE - WG0, True) for j in ring]
+
+    place_f = [[buf.at[k] for buf in (rb0, rb1, rb2)] for k in range(2)]
+    place_m = [[buf.at[k] for buf in (mb0, mb1, mb2)] for k in (0, 1, 2, 0)]
 
     class Reduce:
-        def __init__(self, chunk, distances, count, first, slots, ref):
-            self.first, self.count, self.ref = first, count, ref
+        def __init__(self, chunk, place, ref, chan, first, count, slots):
+            self.ref = ref
             send, recv = rs_send.at[chunk], rs_recv.at[chunk]
             q = count // 4
             cut = q // 32 * 16
             rest = q - cut
-            bufs = [buf.at[chunk % 2] for buf in (rb0, rb1, rb2)]
-            used = [0, 0, 0]
-            k = 0
-
-            def place(level, size):
-                at = used[level]
-                used[level] += size
-                return bufs[level].at[at : at + size, :]
-
-            def rows(part, start, size):
-                return first + part * q + start, size
-
-            def copy(chan, rows, cols, dst, device):
-                nonlocal k
-                k += 1
-                return remote(ref(chan, *rows, cols), dst, send.at[k - 1], recv.at[k - 1], device)
-
-            self.s0, self.s1, self.s2, self.s3 = [], [], [], []
-            near_x, far_x = quarter, y_bit * 2 + 1 - x_bit
+            chans = pl.ds(0, n_chan) if chan is None else pl.ds(chan, 1)
+            n = n_chan if chan is None else 1
+            far_x = y_bit * 2 + 1 - x_bit
             far_y = (1 - y_bit) * 2 + x_bit
-            for j in distances:
-                chan = lax.rem(c + j, n_chan)
-                whole = first, count
-                buf = place(0, count)
-                self.s0.append((chan, first, count, buf, copy(chan, whole, theirs, buf, core_dev)))
-                for part in range(2):
-                    buf = place(1, cut)
-                    self.s1.append((
-                        chan, first + (part * 2 + x_bit) * q, cut, buf,
-                        copy(chan, rows(part * 2 + 1 - x_bit, 0, cut), mine, buf, x_dev),
-                    ))
-                    buf = place(1, rest)
-                    self.s1.append((
-                        chan, first + (y_bit * 2 + part) * q + cut, rest, buf,
-                        copy(chan, rows((1 - y_bit) * 2 + part, cut, rest), mine, buf, y_dev),
-                    ))
-                buf = place(2, cut)
-                self.s2.append((
-                    chan, first + quarter * q, cut, buf,
-                    copy(chan, rows(far_y, 0, cut), mine, buf, y_dev),
-                ))
-                buf = place(2, rest)
-                self.s2.append((
-                    chan, first + quarter * q + cut, rest, buf,
-                    copy(chan, rows(far_x, cut, rest), mine, buf, x_dev),
-                ))
-                if j:
-                    self.s3.append(
-                        copy(chan, rows(quarter, 0, q), mine, slots.at[j - 1], (b, chan))
-                    )
-            self.sent = [item[-1] for item in self.s0 + self.s1 + self.s2] + self.s3
+
+            def item(k, level, at, part, keep, start, size, cols, device):
+                buf = place[level].at[:n, at : at + size, :]
+                src = ref.at[chans, span(first + part * q + start, size), cols]
+                to = chans, span(first + keep * q + start, size)
+                return to, buf, size, remote(src, buf, send.at[k], recv.at[k], device)
+
+            whole = place[0].at[:n, :count, :]
+            src = ref.at[chans, first : first + count, theirs]
+            self.s0 = [(
+                (chans, pl.ds(first, count)), whole, count,
+                remote(src, whole, send.at[0], recv.at[0], core_dev),
+            )]
+            self.s1 = []
+            for k in range(2):
+                self.s1.append(item(
+                    1 + k, 1, k * cut, k * 2 + 1 - x_bit, k * 2 + x_bit, 0, cut, mine, x_dev))
+                self.s1.append(item(
+                    3 + k, 1, 2 * cut + k * rest, (1 - y_bit) * 2 + k, y_bit * 2 + k, cut, rest,
+                    mine, y_dev))
+            self.s2 = [
+                item(5, 2, 0, far_y, quarter, 0, cut, mine, y_dev),
+                item(6, 2, cut, far_x, quarter, cut, rest, mine, x_dev),
+            ]
+            own = span(first + quarter * q, q)
+            self.s3 = [
+                remote(
+                    ref.at[lax.rem(c + j, n_chan), own, mine], slots.at[j - 1],
+                    send.at[6 + j], recv.at[6 + j], (b, lax.rem(c + j, n_chan)),
+                )
+                for j in range(1, n_chan)
+                if chan is None or chunk == j
+            ]
+            self.sent = [it[-1] for it in self.s0 + self.s1 + self.s2] + self.s3
 
         def add(self, items):
-            for chan, start, size, buf, copy in items:
+            for (chans, rows), buf, size, copy in items:
                 copy.wait_recv()
-                for at in range(0, size, 96):
-                    n = min(96, size - at)
-                    here = self.ref(chan, start + at, n, mine)
-                    here[...] = (here[...].astype(F32) + buf[at : at + n, :].astype(F32)).astype(BF)
+                step = 96 if buf.shape[0] == 1 else 16
+                for at in range(0, size, step):
+                    n = min(step, size - at)
+                    here = self.ref.at[chans, span(rows.start + at, n), mine]
+                    here[...] = here[...] + buf[:, at : at + n, :]
 
         def to_core(self):
             for item in self.s0:
@@ -319,7 +331,7 @@
                 copy.wait_send()
 
     class Spread:
-        def __init__(self, chunk, ref, first, count, slots, recvs, dest, dest_first, ex_at):
+        def __init__(self, chunk, ref, first, count, slots, recvs, dest, dest_first, ex_at, turns=False):
             self.ref, self.first, self.q = ref, first, count // 4
             self.slots, self.recvs, self.dest = slots, recvs, dest
             send, recv = fin_send.at[chunk], fin_recv.at[chunk]
@@ -327,8 +339,20 @@
             ref = dest.at[self.at, mine]
             self.copies = [
                 remote(ref, ref, send.at[k], recv.at[k], device)
-                for k, device in enumerate((x_dev, y_dev, diag_dev))
+                for k, device in enumerate((x_dev, y_dev) if turns else (x_dev, y_dev, diag_dev))
             ]
+            self.p2 = []
+            if turns:
+                cut = self.q // 32 * 16
+                parts = (
+                    (y_bit * 2 + 1 - x_bit, 0, cut, y_dev),
+                    ((1 - y_bit) * 2 + x_bit, cut, self.q - cut, x_dev),
+                )
+                for k, (part, start, size, device) in enumerate(parts):
+                    half_ref = dest.at[span(dest_first + part * self.q + start, size), mine]
+                    self.p2.append(remote(
+                        half_ref, half_ref, send.at[4 + k], recv.at[4 + k], device
+                    ))
             ref_all = dest.at[dest_first : dest_first + count, mine]
             self.last = remote(ref_all, ref_all, send.at[3], recv.at[3], core_dev)
             self.extra = []
@@ -341,7 +365,7 @@
         def total(self):
             for copy in self.recvs:
                 copy.wait_recv()
-            v = self.ref(c, self.first + quarter * self.q, self.q, mine)[...].astype(F32)
+            v = self.ref[c, span(self.first + quarter * self.q, self.q), mine].astype(F32)
             for j in range(n_chan - 1):
                 v = v + self.slots[j].astype(F32)
             self.dest[self.at, mine] = v.astype(BF)
@@ -353,44 +377,61 @@
             for copy in self.copies:
                 copy.start()
 
-        def cross(self):
+        def turn(self):
             for copy in self.copies:
                 copy.wait_recv()
+            for copy in self.p2:
+                copy.start()
+
+        def cross(self):
+            for copy in self.p2 or self.copies:
+                copy.wait_recv()
             self.last.start()
 
         def done(self):
             self.last.wait_recv()
-            for copy in self.copies + [self.last]:
+            for copy in self.copies + self.p2 + [self.last]:
                 copy.wait_send()
 
-    reduce_f = [Reduce(j, [j], PIECE - WG0, WG0, zbf, in_w) for j in range(n_chan)]
-    reduce_a = Reduce(n_chan, range(n_chan), WG0 - MA0, MA0, zba, in_w)
-    reduce_b = Reduce(n_chan + 1, range(n_chan), MA0, 0, zbb, in_dm)
+    f_rows = PIECE - WG0
+    reduce_f = [
+        Reduce(j, place_f[j % 2], w, lax.rem(c + j, n_chan), WG0, f_rows, zbf)
+        for j in range(n_chan)
+    ]
+    reduce_o = Reduce(n_chan, place_m[0], w, None, WO0, WG0 - WO0, zbm.at[0])
+    reduce_g = Reduce(n_chan + 1, place_m[1], w, None, MA0, WO0 - MA0, zbm.at[1])
+    reduce_v = Reduce(n_chan + 2, place_m[2], dm, None, 0, 2 * nch, zbm.at[2])
+    reduce_k = Reduce(
+        n_chan + 3, place_m[3], dm, None, 2 * nch, MA0 - 2 * nch,
+        zbm.at[3, :, : (MA0 - 2 * nch) // 4],
+    )
     spread_f = Spread(
-        0, in_w, WG0, PIECE - WG0, zbf, [copy for r in reduce_f for copy in r.s3], dgu, 0, 0
+        0, w, WG0, f_rows, zbf, [copy for r in reduce_f for copy in r.s3], dgu, 0, 0, True
     )
-    spread_a = Spread(1, in_w, MA0, WG0 - MA0, zba, reduce_a.s3, mixf, MA0, (PIECE - WG0) // 4)
-    spread_b = Spread(2, in_dm, 0, MA0, zbb, reduce_b.s3, mixf, 0, (PIECE - MA0) // 4)
+    at = [f_rows // 4 + k * (nch // 2) for k in range(4)]
+    spread_o = Spread(1, w, WO0, WG0 - WO0, zbm.at[0], reduce_o.s3, mixf, WO0, at[0])
+    spread_g = Spread(2, w, MA0, WO0 - MA0, zbm.at[1], reduce_g.s3, mixf, MA0, at[1])
+    spread_v = Spread(3, dm, 0, 2 * nch, zbm.at[2], reduce_v.s3, mixf, 0, at[2])
+    spread_k = Spread(
+        4, dm, 2 * nch, MA0 - 2 * nch, zbm.at[3, :, : (MA0 - 2 * nch) // 4], reduce_k.s3, mixf,
+        2 * nch, at[3],
+    )
 
     for copy in load_first:
         copy.wait()
-    for g in gather_a:
-        g.along()
     par_copies = exchange(parx, par_send, par_recv)
     for copy in par_copies:
         copy.start()
+    for g in gather_a:
+        g.along()
     for copy in load_second:
         copy.wait()
-    for g in gather_b:
-        g.along()
     hw = hid.shape[1]
     load_gate.wait()
     w[c, WG0 : WG0 + hw, :] = hid[:width, :].T
     load_up.wait()
     w[c, WG0 + hw : WD0, :] = dgu[:width, :hw].T
     load_down.wait()
-    for g in gather_f:
-        g.along()
     lane_r = lax.broadcasted_iota(jnp.int32, (half, half), 0) // HEAD_CH
     lane_c = lax.broadcasted_iota(jnp.int32, (half, half), 1) // HEAD_CH
     ones[...] = jnp.where(lane_r == lane_c, 1.0 / (2 * HEAD_CH), 0.0).astype(BF)
@@ -418,13 +459,56 @@
     live_rows = slot_limit - offset
     not_start = jnp.where(offset == 0, 0.0, 1.0).astype(F32)
 
+    def section(k):
+        return jnp.concatenate(
+            [w[cc, SECTION[k] : SECTION[k] + 96, :] for cc in range(n_chan)], axis=0
+        )
+
+    def out_rows(k):
+        return jnp.concatenate(
+            [w[cc, WO0 + 96 * k : WO0 + 96 * k + 96, :] for cc in range(n_chan)], axis=0
+        )
+
+    def order_tokens(i):
+        part = jnp.concatenate([fin[at, :] for at in blocks(i)], axis=0)
+        tok[rows_of(i, TM), :] = dot(swap[...], part, 1, 0).astype(BF)
+
+    def order_seed(i):
+        part = jnp.concatenate(
+            [
+                dm[k, span(seg_len * m + SEGS * i, SEGS), :]
+                for k in range(n_chan)
+                for m in range(SEGS // n_chan)
+            ],
+            axis=0,
+        ).astype(F32)
+        k = lax.broadcasted_iota(jnp.int32, (TM, 1), 0)
+        place = k // SEGS * seg_len + lax.rem(k, SEGS) + SEGS * i
+        part = (part * jnp.where(place < live_rows, 1.0, 0.0)).astype(BF)
+        sd[rows_of(i, TM), :] = dot(swap[...], part, 1, 0).astype(BF)
+
+    load_tok.wait()
+    tiles(n_tiles, order_tokens)
+    for g in gather_a:
+        g.plane()
+    for g in gather_b + gather_o + [gather_f[0], gather_f[2]]:
+        g.along()
+    for g in gather_a:
+        g.turn()
+    for g in gather_b:
+        g.plane()
+    for g in gather_a:
+        g.cross()
+    for g in gather_a:
+        g.ready()
+
     for copy in par_copies:
         copy.wait()
     par = parx[0] + parx[1] + parx[2] + parx[3]
     bias = par[0:1, :]
     cos1, sin1 = par[1:2, :], par[2:3, :]
     gain_r, gain_i = par[3:4, :], par[4:5, :]
-    rms_gain = rms_ref[...]
+    rms_gain = jnp.concatenate([rms_ref[k : k + 1, :] for k in range(width // 128)], axis=1)
     cos16 = jnp.broadcast_to(cos1, (SEGS, half))
     sin16 = jnp.broadcast_to(sin1, (SEGS, half))
 
@@ -437,42 +521,6 @@
 
     seg_cos, seg_sin = power(seg_len)
     all_cos, all_sin = power(n_rows)
-
-    def section(k):
-        return jnp.concatenate(
-            [w[cc, SECTION[k] : SECTION[k] + 96, :] for cc in range(n_chan)], axis=0
-        )
-
-    def out_rows(k):
-        return jnp.concatenate(
-            [w[cc, WO0 + 96 * k : WO0 + 96 * k + 96, :] for cc in range(n_chan)], axis=0
-        )
-
-    def order_tokens(i):
-        part = jnp.concatenate([fin[at, :] for at in blocks(i)], axis=0)
-        tok[rows_of(i, TM), :] = dot(swap[...], part, 1, 0).astype(BF)
-
-    def order_seed(i):
-        part = jnp.concatenate([dm[at, :] for at in blocks(i)], axis=0).astype(F32)
-        k = lax.broadcasted_iota(jnp.int32, (TM, 1), 0)
-        place = k // SEGS * seg_len + lax.rem(k, SEGS) + SEGS * i
-        part = (part * jnp.where(place < live_rows, 1.0, 0.0)).astype(BF)
-        sd[rows_of(i, TM), :] = dot(swap[...], part, 1, 0).astype(BF)
-
-    load_tok.wait()
-    tiles(n_tiles, order_tokens)
-    for g in gather_a:
-        g.plane()
-    load_cot.wait()
-    tiles(n_tiles, order_seed)
-    for g in gather_b:
-        g.plane()
-    for g in gather_a:
-        g.turn()
-    for g in gather_a:
-        g.cross()
-    for g in gather_a:
-        g.ready()
 
     def project(i):
         rows = rows_of(i, TM)
@@ -484,10 +532,9 @@
         put(om, rows, 0, 1.0 / (1.0 + jnp.exp(dot(x, section(2), 1, 1) + bias)))
 
     tiles(n_tiles, project, {
-        1: [g.turn for g in gather_b],
-        3: [g.cross for g in gather_b],
+        0: [g.plane for g in gather_o],
+        2: [g.turn for g in gather_b],
     })
-    gather_f[0].plane()
 
     def strided(t):
         return span(t * SEGS, SEGS)
@@ -531,21 +578,18 @@
     carx[c, 1:2, :] = ei
     carx[c, 2:3, :] = total * all_cos * not_start
     carx[c, 3:4, :] = total * all_sin * not_start
-    car_copies = exchange(carx, car_send, car_recv)
-    for copy in car_copies:
-        copy.start()
+    to_later, from_earlier = chain(carx, car_send, car_recv, True)
+    to_later()
     for g in gather_b:
-        g.ready()
-
-    def project_gate(i):
-        rows = rows_of(i, TM)
-        x = tok[rows, :]
-        for k in range(2):
-            pg[rows, k * half : (k + 1) * half] = dot(x, section(3 + k), 1, 1)
-
-    tiles(n_tiles, project_gate, {1: [gather_f[1].plane], 2: [gather_f[0].turn]})
-    for copy in car_copies:
+        g.cross()
+    for g in gather_o:
+        g.turn()
+    gather_f[0].plane()
+    for copy in load_cot:
         copy.wait()
+    tiles(n_tiles, order_seed)
+    from_earlier()
+    gather_f[1].along()
     cr, ci = zrow, zrow
     for k in range(n_chan - 1):
         ar, ai = carx[k, 2:3, :], carx[k, 3:4, :]
@@ -568,6 +612,18 @@
         return f * tr + o * vr, f * ti + o * vi
 
     lax.fori_loop(0, seg_len, second, (seg[2], seg[3]), unroll=4)
+    for g in gather_b:
+        g.ready()
+
+    def project_gate(i):
+        rows = rows_of(i, TM)
+        x = tok[rows, :]
+        for k in range(2):
+            pg[rows, k * half : (k + 1) * half] = dot(x, section(3 + k), 1, 1)
+
+    tiles(n_tiles, project_gate, {2: [g.cross for g in gather_o]})
+    for g in gather_o:
+        g.ready()
 
     def mixer_out(i):
         rows = rows_of(i, TM)
@@ -596,10 +652,9 @@
         dff[rows, :] = jnp.zeros((TM, width), F32)
 
     tiles(n_tiles, mixer_out, {
-        0: [gather_f[0].cross],
-        1: [gather_f[1].turn, gather_f[2].plane],
-        2: [gather_f[0].ready, gather_f[1].cross],
-        3: [gather_f[2].turn],
+        0: [gather_f[0].turn],
+        1: [gather_f[2].plane],
+        3: [gather_f[0].cross],
     })
 
     for j in range(n_chan):
@@ -622,15 +677,24 @@
             dff[rows, :] += dot(dgu[rows, :], w[cc, WG0:WD0, :], 1, 0)
 
         if j == 0:
-            tiles(n_tiles, feed, {0: [gather_f[2].cross], 1: [gather_f[1].ready]})
+            tiles(n_tiles, feed, {
+                0: [gather_f[2].turn],
+                1: [gather_f[1].plane],
+                3: [gather_f[2].cross],
+            })
             for g in gather_f:
                 g.along_free()
+            gather_f[0].ready()
         else:
             before = reduce_f[j - 1]
             older = [reduce_f[j - 2]] if j > 1 else []
-            if j == n_chan - 1:
+            if j > 1:
                 gather_f[j - 1].ready()
-            tiles(n_tiles, feed, {1: [r.turn for r in older], 2: [before.to_plane]})
+            tiles(n_tiles, feed, {
+                1: [r.turn for r in older],
+                2: [before.to_plane],
+                **({0: [gather_f[1].turn], 3: [gather_f[1].cross]} if j == 1 else {}),
+            })
             gather_f[j - 1].free()
         for k in range(2):
             w[cc, WG0 + hw * k : WG0 + hw * (k + 1), :] = dot(
@@ -657,7 +721,7 @@
         )
         dff[rows, :] = dres
         low = dres.astype(BF)
-        dm[rows, :] = low
+        dm[i * TM // per, span(lax.rem(i * TM, per), TM), :] = low
         dr = dot(low, out_rows(0), 1, 1)
         di = dot(low, out_rows(1), 1, 1)
         xr, xi = xh[rows, :half], xh[rows, half:]
@@ -688,25 +752,12 @@
         dff[rows, :] = acc
 
     tiles(n_tiles, mixer_back, {
-        0: [reduce_f[-2].turn],
-        1: [reduce_f[-1].to_plane],
-        3: [reduce_f[-2].along],
+        1: [reduce_f[-2].turn, reduce_f[-1].to_plane],
     })
     out_copy = pltpu.make_async_copy(fin, out_hbm, store_sem.at[0])
     out_copy.start()
 
-    for g in gather_a + gather_b:
-        g.along_free()
-        g.free()
-    for k in range(4):
-        left = mix[:, k * half : (k + 1) * half] if k < 2 else dp[:, (k + 1) * half : (k + 2) * half]
-        grad = dot(left, dm[:n_rows, :] if k < 2 else tok[...], 0, 0).astype(BF)
-        to = WO0 + 96 * k if k < 2 else SECTION[k + 1]
-        for cc in range(n_chan):
-            w[cc, to : to + 96, :] = grad[96 * cc : 96 * cc + 96, :]
-        if k == 1:
-            reduce_f[-1].turn()
-    reduce_a.to_core()
+    reduce_f[-1].turn()
 
     def first_back(k, carry):
         qr, qi = carry
@@ -736,18 +787,31 @@
     er, ei = fold_back(zrow, zrow, False)
     carb[c, 0:1, :] = er * not_start
     carb[c, 1:2, :] = ei * not_start
-    car_copies = exchange(carb, cab_send, cab_recv)
-    for copy in car_copies:
-        copy.start()
-
+    carb[c, 2:4, :] = carx[c, 2:4, :]
+    to_earlier, from_later = chain(carb, cab_send, cab_recv, False)
+    to_earlier()
+    reduce_f[-2].along()
+
+    for g in gather_a + gather_b + gather_o:
+        g.along_free()
+        g.free()
+    d_mixed = jnp.concatenate([dm[k, :per, :] for k in range(n_chan)], axis=0)
+    for k in range(4):
+        left = mix[:, k * half : (k + 1) * half] if k < 2 else dp[:, (k + 1) * half : (k + 2) * half]
+        grad = dot(left, d_mixed if k < 2 else tok[...], 0, 0).astype(BF)
+        to = WO0 + 96 * k if k < 2 else SECTION[k + 1]
+        for cc in range(n_chan):
+            w[cc, to : to + 96, :] = grad[96 * cc : 96 * cc + 96, :]
+        if k == 1:
+            reduce_o.to_core()
+    reduce_o.to_plane()
+    reduce_g.to_core()
+
+    from_later()
     reduce_f[-1].along()
-    reduce_a.to_plane()
-
-    for copy in car_copies:
-        copy.wait()
     cr, ci = zrow, zrow
     for k in range(n_chan - 1, 0, -1):
-        ar, ai = carx[k, 2:3, :], -carx[k, 3:4, :]
+        ar, ai = carb[k, 2:3, :], -carb[k, 3:4, :]
         nr = ar * cr - ai * ci + carb[k, 0:1, :]
         ni = ar * ci + ai * cr + carb[k, 1:2, :]
         cr = jnp.where(k > c, nr, cr)
@@ -789,20 +853,23 @@
             )
         )
 
+    reduce_g.to_plane()
     tiles(n_tiles, project_back)
+    for k in range(3):
+        grad = dot(dp[:, k * half : (k + 1) * half], tok[...], 0, 0).astype(BF)
+        for cc in range(n_chan):
+            dm[cc, 96 * k : 96 * k + 96, :] = grad[96 * cc : 96 * cc + 96, :]
+        if k == 1:
+            reduce_v.to_core()
+            reduce_o.turn()
     small = jnp.concatenate(
         [jnp.sum(sgrad[k], axis=0, keepdims=True) for k in range(3)]
         + [jnp.zeros((29, width), F32)],
         axis=0,
     ).astype(BF)
     for cc in range(n_chan):
-        dm[MA0 * cc + PAD0 : MA0 * (cc + 1), :] = small
-    for k in range(3):
-        grad = dot(dp[:, k * half : (k + 1) * half], tok[...], 0, 0).astype(BF)
-        for cc in range(n_chan):
-            at = MA0 * cc + 96 * k
-            dm[at : at + 96, :] = grad[96 * cc : 96 * cc + 96, :]
-    reduce_b.to_core()
+        dm[cc, PAD0:MA0, :] = small
+    reduce_k.to_core()
     def d_tokens(i):
         rows = rows_of(i, TM)
         acc = dff[rows, :]
@@ -815,27 +882,33 @@
             res[at, :] = done[SEGS * k : SEGS * (k + 1), :]
 
     tiles(n_tiles, d_tokens, {
-        0: [spread_f.total, reduce_a.turn],
-        2: [reduce_b.to_plane],
-        3: [spread_f.cross],
+        1: [reduce_v.to_plane, reduce_g.turn],
+        2: [reduce_o.along, reduce_k.to_plane],
     })
     gtok_copy = pltpu.make_async_copy(res, gtok_hbm, store_sem.at[1])
     gtok_copy.start()
-    reduce_a.along()
-    reduce_b.turn()
+    reduce_v.turn()
+    reduce_k.turn()
+    spread_f.total()
+    reduce_g.along()
+    reduce_v.along()
+    reduce_k.along()
+    spread_o.total()
+    spread_f.turn()
+    spread_g.total()
+    spread_v.total()
+    spread_k.total()
+    spread_f.cross()
+    for sp in (spread_o, spread_g, spread_v, spread_k):
+        sp.cross()
     spread_f.done()
     g_copies = [pltpu.make_async_copy(dgu, g_hbm.at[WG0:PIECE, :], store_sem.at[2])]
     g_copies[0].start()
-    spread_a.total()
-    reduce_b.along()
-    spread_a.cross()
-    spread_b.total()
-    spread_a.done()
-    spread_b.cross()
-    spread_b.done()
+    for sp in (spread_o, spread_g, spread_v, spread_k):
+        sp.done()
     g_copies.append(pltpu.make_async_copy(mixf, g_hbm.at[:WG0, :], store_sem.at[3]))
     g_copies[1].start()
-    for r in reduce_f + [reduce_a, reduce_b]:
+    for r in reduce_f + [reduce_o, reduce_g, reduce_v, reduce_k]:
         r.free()
     for copy in [out_copy, gtok_copy] + g_copies:
         copy.wait()
@@ -943,7 +1016,7 @@
             pltpu.SemaphoreType.DMA((7,)),
             pltpu.SemaphoreType.DMA((9,)),
         ],
-        compiler_params=pltpu.CompilerParams(vmem_limit_bytes=48 * 2**20),
+        compiler_params=pltpu.CompilerParams(vmem_limit_bytes=60 * 2**20),
         name="place",
     )(g, grad_tokens, block_out)
 
@@ -977,7 +1050,7 @@
             full16, full16, full32, pltpu.VMEM((half // 128, rows, 128), F32), full32, tiles32,
             full32, half32, full32, full16, full16, tiles32, full32,
             pltpu.VMEM((rows, hw), BF), pltpu.VMEM((PIECE - WG0, 2 * hw), BF),
-            pltpu.VMEM((max(rows, n_chan * MA0), width), BF), pltpu.VMEM((rows, 5 * half), BF),
+            pltpu.VMEM((n_chan, MA0, width), BF), pltpu.VMEM((rows, 5 * half), BF),
             pltpu.VMEM((half, half), BF),
             pltpu.VMEM((TM, TM), BF),
             pltpu.VMEM((n_chan, 8, half), F32),
@@ -986,25 +1059,27 @@
             pltpu.VMEM((4, SEGS, half), F32),
             pltpu.VMEM((3, 8, width), F32),
             pltpu.VMEM((SEGS, half), F32),
-            pltpu.VMEM((2, n_chan * (WG0 - MA0), half), BF),
-            pltpu.VMEM((2, n_chan * (WG0 - MA0) // 2, half), BF),
-            pltpu.VMEM((2, n_chan * (WG0 - MA0) // 4, half), BF),
+            pltpu.VMEM((2, 1, PIECE - WG0, half), BF),
+            pltpu.VMEM((2, 1, (PIECE - WG0) // 2, half), BF),
+            pltpu.VMEM((2, 1, (PIECE - WG0) // 4, half), BF),
+            pltpu.VMEM((3, n_chan, WG0 - WO0, half), BF),
+            pltpu.VMEM((3, n_chan, (WG0 - WO0) // 2, half), BF),
+            pltpu.VMEM((3, n_chan, (WG0 - WO0) // 4, half), BF),
             pltpu.VMEM((n_chan - 1, (PIECE - WG0) // 4, half), BF),
-            pltpu.VMEM((n_chan - 1, (WG0 - MA0) // 4, half), BF),
-            pltpu.VMEM((n_chan - 1, MA0 // 4, half), BF),
+            pltpu.VMEM((4, n_chan - 1, (WG0 - WO0) // 4, half), BF),
             pltpu.VMEM((WG0, width), BF),
-            pltpu.VMEM((n_extra, PIECE // 4, half) if n_batch > 8 else (1, 16, 128), BF),
+            pltpu.VMEM((n_extra, (PIECE + 64) // 4, half) if n_batch > 8 else (1, 16, 128), BF),
             pltpu.VMEM((8, half), F32),
-            pltpu.SemaphoreType.DMA((6 + 6 * nch // HEAD_CH,)),
+            pltpu.SemaphoreType.DMA((5 + n_chan + 6 * nch // HEAD_CH,)),
             pltpu.SemaphoreType.DMA((4,)),
         ]
-        + [pltpu.SemaphoreType.DMA((n_chan - 1,))] * 6
-        + [pltpu.SemaphoreType.DMA((3 * (n_chan - 1), 9))] * 2
-        + [pltpu.SemaphoreType.DMA((n_chan + 2, 8 * n_chan))] * 2
-        + [pltpu.SemaphoreType.DMA((3, 4))] * 2
-        + [pltpu.SemaphoreType.DMA((3, n_extra))] * 2,
+        + [pltpu.SemaphoreType.DMA((n_chan,))] * 6
+        + [pltpu.SemaphoreType.DMA((4 * (n_chan - 1), 9))] * 2
+        + [pltpu.SemaphoreType.DMA((n_chan + 4, 10))] * 2
+        + [pltpu.SemaphoreType.DMA((5, 6))] * 2
+        + [pltpu.SemaphoreType.DMA((5, n_extra))] * 2,
         compiler_params=pltpu.CompilerParams(
-            collective_id=0, has_side_effects=True, vmem_limit_bytes=60 * 2**20
+            collective_id=0, has_side_effects=True, vmem_limit_bytes=62 * 2**20
         ),
         cost_estimate=pl.CostEstimate(
             flops=34 * 10**9, bytes_accessed=3 * 10**7, transcendentals=0
@@ -1019,7 +1094,7 @@
 ):
     g, grad_tokens, block_out = main_call(
         (w_in.T, w_forget.T, w_outgate.T, w_out, w_gate, w_up, w_down), tokens, cotangent,
-        (b_forget[None], rotation[None], gn_gain[None], rms_gain[None]), buckets, lengths,
+        (b_forget[None], rotation[None], gn_gain[None], rms_gain.reshape(-1, 128)), buckets, lengths,
     )
     (
         grad_w_in, grad_w_forget, grad_b, grad_rot, grad_w_outgate, grad_gn, grad_w_out, grad_rms,

time: 183 us -> 145 us (0.79)
  Pallas kernels: 177 us -> 143 us
  local copies, waits for them, and re-layouts: 4.47 us -> 0 us
    pallas_call x1, Pallas kernels: 169 us -> 136 us  [main_call(): pl.pallas_call(functools.partial(main_kernel, n_batch, n_chan), out_shape...]
    unnamed x4 -> x0, local copies, waits for them, and re-layouts: 3.21 us -> none
where the time goes in v3:
time: 145 us
  Pallas kernels  143 us (99%)
  between operations  1.49 us (1%)
    pallas_call x1, Pallas kernels, main_call(): pl.pallas_call(functools.partial(main_kernel, n_batch, n_chan), out_shape...  136 us
    pallas_call x1, Pallas kernels, post_call(): pl.pallas_call(post_kernel, out_shape=[jax.ShapeDtypeStruct(shape, F32) f...  7.19 us

profile of v3, /device:TPU:0, one launch (start us, length us, event | category | flops | bytes accessed | tf_op | source)
XLA Modules:
  0.0 145.0 jit_solution(14573633811942486582)
XLA Ops:
  1.3 136.3 %block.1 = (bf16[1856,768]{1,0:T(8,128)(2,1)}, f32[1024,768]{1,0:T(8,128)}, bf16[1024,768]{1,0:T(8,128)(2,1)}) custom-call(bf16[192,768]{1,0:T(8,128)(2,1)} %bitcast.16, bf16[96,768]{1,0:T(8,128)(2,1)} %bitcast.19, bf16[192,768]{1,0:T(8,128)(2,1)} %bitcast.17, bf16[192,768]{1,0:T(8,128)(2,1)} %wout_hbm.1, bf16[768,384]{1,0:T(8,128)(2,1)} %wgate_hbm.1, ...), custom_call_target="tpu_custom_call" | custom-call | flops 33999998976 | bytes 30000000 | tf_op jit(solution)/shard_map/block/pallas_call | solution.py:1039
  137.6 7.2 %place.1 = (f32[192,768]{1,0:T(8,128)}, f32[96,768]{1,0:T(8,128)}, f32[1,96]{1,0:T(1,128)}, f32[1,96]{1,0:T(1,128)}, f32[192,768]{1,0:T(8,128)}, /*index=5*/f32[...) custom-call(bf16[1856,768]{1,0:T(8,128)(2,1)} %get-tuple-element.29., ...), custom_call_target="tpu_custom_call" | custom-call | tf_op jit(solution)/shard_map/place/pallas_call | solution.py:1005

commit v4 on v3

--- a/solution.py
+++ b/solution.py
@@ -13,6 +13,7 @@
 HEAD_CH = 32
 SEGS = 16
 TM = SEGS * SEGS
+ORDER = (0, 1, 3, 2)
 PAD0, MA0, WO0, WG0, WD0, PIECE = 288, 320, 512, 704, 1472, 1856
 SECTION = (0, 96, 192, 320, 416)
 
@@ -64,7 +65,7 @@
     g_hbm, gtok_hbm, out_hbm,
     w, tok, sd, pv, om, pg, ws, xh, rstd, res, fin, mix, out, dff, hid, dgu, dm, dp,
     ones, swap, parx, carx, carb, seg, sgrad, seg_prod,
-    rb0, rb1, rb2, mb0, mb1, mb2, zbf, zbm, mixf, extra,
+    rb0, rb1, rb2, mb0, mb1, mb2, zbf, zbq, zbm, mixf, extra,
     par_own,
     load_sem, store_sem, par_send, par_recv, car_send, car_recv, cab_send, cab_recv,
     ag_send, ag_recv, rs_send, rs_recv, fin_send, fin_recv, ex_send, ex_recv,
@@ -198,6 +199,7 @@
             self.c1 = copy(3, src, own, core_dev)
             if turns:
                 cut = count // 4 // 32 * 16
+                cut = cut if unit // (n_chan - 1) % 2 else count // 4 - cut
                 rest = count // 4 - cut
                 self.p2 = [
                     copy(4, src, self.rows(from_x, 0, cut), y_dev),
@@ -244,20 +246,22 @@
                 copy.wait_send()
 
     ring = range(1, n_chan)
-    gather_a = [Gather(j - 1, j, 0, MA0, False) for j in ring]
+    gather_v = [Gather(j - 1, j, 0, 2 * nch, True) for j in ring]
+    gather_k = [Gather(11 + j, j, 2 * nch, MA0 - 2 * nch, True) for j in ring]
     gather_b = [Gather(2 + j, j, MA0, WO0 - MA0, True) for j in ring]
     gather_o = [Gather(5 + j, j, WO0, WG0 - WO0, True) for j in ring]
-    gather_f = [Gather(8 + j, j, WG0, PIECE - WG0, True) for j in ring]
+    gather_f = [Gather(8 + j, j, WG0, PIECE - WG0, True) for j in ORDER[1:]]
 
     place_f = [[buf.at[k] for buf in (rb0, rb1, rb2)] for k in range(2)]
     place_m = [[buf.at[k] for buf in (mb0, mb1, mb2)] for k in (0, 1, 2, 0)]
 
     class Reduce:
-        def __init__(self, chunk, place, ref, chan, first, count, slots):
-            self.ref = ref
+        def __init__(self, chunk, place, ref, dist, first, count, slots, late=False):
+            chan = None if dist is None else lax.rem(c + dist, n_chan)
+            self.ref, self.slots = ref, slots
             send, recv = rs_send.at[chunk], rs_recv.at[chunk]
             q = count // 4
-            cut = q // 32 * 16
+            cut = q // 32 * 16 if chunk % 2 else q - q // 32 * 16
             rest = q - cut
             chans = pl.ds(0, n_chan) if chan is None else pl.ds(chan, 1)
             n = n_chan if chan is None else 1
@@ -283,19 +287,39 @@
                 self.s1.append(item(
                     3 + k, 1, 2 * cut + k * rest, (1 - y_bit) * 2 + k, y_bit * 2 + k, cut, rest,
                     mine, y_dev))
-            self.s2 = [
-                item(5, 2, 0, far_y, quarter, 0, cut, mine, y_dev),
-                item(6, 2, cut, far_x, quarter, cut, rest, mine, x_dev),
+            self.s2 = []
+            if not (late and dist):
+                self.s2 = [
+                    item(5, 2, 0, far_y, quarter, 0, cut, mine, y_dev),
+                    item(6, 2, cut, far_x, quarter, cut, rest, mine, x_dev),
+                ]
+            own = span(first + quarter * q, q)
+            self.pairs = [(first + (k * 2 + x_bit) * q, cut, k * cut) for k in range(2)]
+            self.pairs += [
+                (first + (y_bit * 2 + k) * q + cut, rest, 2 * cut + k * rest) for k in range(2)
             ]
-            own = span(first + quarter * q, q)
-            self.s3 = [
-                remote(
-                    ref.at[lax.rem(c + j, n_chan), own, mine], slots.at[j - 1],
-                    send.at[6 + j], recv.at[6 + j], (b, lax.rem(c + j, n_chan)),
-                )
-                for j in range(1, n_chan)
-                if chan is None or chunk == j
-            ]
+            if late and dist:
+                self.s3 = [
+                    remote(
+                        ref.at[chan, span(start, size), mine],
+                        slots.at[dist // 2, at : at + size, :],
+                        send.at[7 + k], recv.at[7 + k], (b, chan),
+                    )
+                    for k, (start, size, at) in enumerate(self.pairs)
+                ]
+            elif dist:
+                self.s3 = [remote(
+                    ref.at[chan, own, mine], slots, send.at[7], recv.at[7], (b, chan)
+                )]
+            else:
+                self.s3 = [
+                    remote(
+                        ref.at[lax.rem(c + j, n_chan), own, mine], slots.at[j - 1],
+                        send.at[6 + j], recv.at[6 + j], (b, lax.rem(c + j, n_chan)),
+                    )
+                    for j in range(1, n_chan)
+                    if dist is None
+                ]
             self.sent = [it[-1] for it in self.s0 + self.s1 + self.s2] + self.s3
 
         def add(self, items):
@@ -314,6 +338,30 @@
         def to_plane(self):
             self.add(self.s0)
             for item in self.s1:
+                item[-1].start()
+
+        def pair(self):
+            self.add(self.s1)
+
+        def send_along(self):
+            for copy in self.s3:
+                copy.start()
+
+        def pair_along(self):
+            self.pair()
+            self.send_along()
+
+        def collect(self, copies):
+            for copy in copies:
+                copy.wait_recv()
+            for start, size, at in self.pairs:
+                for k in range(0, size, 48):
+                    here = span(start + k, 48)
+                    v = self.ref[c, here, mine].astype(F32)
+                    for j in range(self.slots.shape[0]):
+                        v = v + self.slots[j, at + k : at + k + 48, :].astype(F32)
+                    self.ref[c, here, mine] = v.astype(BF)
+            for item in self.s2:
                 item[-1].start()
 
         def turn(self):
@@ -366,8 +414,8 @@
             for copy in self.recvs:
                 copy.wait_recv()
             v = self.ref[c, span(self.first + quarter * self.q, self.q), mine].astype(F32)
-            for j in range(n_chan - 1):
-                v = v + self.slots[j].astype(F32)
+            for j in range(len(self.recvs)):
+                v = v + self.slots[j][...].astype(F32)
             self.dest[self.at, mine] = v.astype(BF)
             for buf, copy in self.extra:
                 copy.start()
@@ -395,22 +443,20 @@
 
     f_rows = PIECE - WG0
     reduce_f = [
-        Reduce(j, place_f[j % 2], w, lax.rem(c + j, n_chan), WG0, f_rows, zbf)
-        for j in range(n_chan)
+        Reduce(k, place_f[k % 2], w, j, WG0, f_rows, zbf if j != 2 else zbq, j != 2)
+        for k, j in enumerate(ORDER)
     ]
-    reduce_o = Reduce(n_chan, place_m[0], w, None, WO0, WG0 - WO0, zbm.at[0])
-    reduce_g = Reduce(n_chan + 1, place_m[1], w, None, MA0, WO0 - MA0, zbm.at[1])
+    reduce_o = Reduce(n_chan, place_m[0], sd, None, 0, WG0 - WO0, zbm.at[0])
+    reduce_g = Reduce(n_chan + 1, place_m[1], w, None, WO0, WO0 - MA0, zbm.at[1])
     reduce_v = Reduce(n_chan + 2, place_m[2], dm, None, 0, 2 * nch, zbm.at[2])
     reduce_k = Reduce(
         n_chan + 3, place_m[3], dm, None, 2 * nch, MA0 - 2 * nch,
         zbm.at[3, :, : (MA0 - 2 * nch) // 4],
     )
-    spread_f = Spread(
-        0, w, WG0, f_rows, zbf, [copy for r in reduce_f for copy in r.s3], dgu, 0, 0, True
-    )
+    spread_f = Spread(0, w, WG0, f_rows, [zbq], reduce_f[-1].s3, dgu, 0, 0, True)
     at = [f_rows // 4 + k * (nch // 2) for k in range(4)]
-    spread_o = Spread(1, w, WO0, WG0 - WO0, zbm.at[0], reduce_o.s3, mixf, WO0, at[0])
-    spread_g = Spread(2, w, MA0, WO0 - MA0, zbm.at[1], reduce_g.s3, mixf, MA0, at[1])
+    spread_o = Spread(1, sd, 0, WG0 - WO0, zbm.at[0], reduce_o.s3, mixf, WO0, at[0])
+    spread_g = Spread(2, w, WO0, WO0 - MA0, zbm.at[1], reduce_g.s3, mixf, MA0, at[1])
     spread_v = Spread(3, dm, 0, 2 * nch, zbm.at[2], reduce_v.s3, mixf, 0, at[2])
     spread_k = Spread(
         4, dm, 2 * nch, MA0 - 2 * nch, zbm.at[3, :, : (MA0 - 2 * nch) // 4], reduce_k.s3, mixf,
@@ -422,7 +468,7 @@
     par_copies = exchange(parx, par_send, par_recv)
     for copy in par_copies:
         copy.start()
-    for g in gather_a:
+    for g in gather_v + gather_k:
         g.along()
     for copy in load_second:
         copy.wait()
@@ -485,21 +531,28 @@
         k = lax.broadcasted_iota(jnp.int32, (TM, 1), 0)
         place = k // SEGS * seg_len + lax.rem(k, SEGS) + SEGS * i
         part = (part * jnp.where(place < live_rows, 1.0, 0.0)).astype(BF)
-        sd[rows_of(i, TM), :] = dot(swap[...], part, 1, 0).astype(BF)
+        sd[i] = dot(swap[...], part, 1, 0).astype(BF)
 
     load_tok.wait()
     tiles(n_tiles, order_tokens)
-    for g in gather_a:
+    for g in gather_v:
         g.plane()
-    for g in gather_b + gather_o + [gather_f[0], gather_f[2]]:
+    for copy in load_cot:
+        copy.wait()
+    tiles(n_tiles, order_seed)
+    for g in gather_k:
+        g.plane()
+    for g in gather_b + gather_o + gather_f[:2]:
         g.along()
-    for g in gather_a:
+    for g in gather_v:
         g.turn()
-    for g in gather_b:
-        g.plane()
-    for g in gather_a:
+    for g in gather_k:
+        g.turn()
+    for g in gather_v:
         g.cross()
-    for g in gather_a:
+    for g in gather_k:
+        g.cross()
+    for g in gather_v:
         g.ready()
 
     for copy in par_copies:
@@ -529,12 +582,16 @@
             pre = dot(x, section(k), 1, 1)
             pv[rows, k * half : (k + 1) * half] = pre
             put(out, rows, k * lt, pre * sigmoid(pre))
-        put(om, rows, 0, 1.0 / (1.0 + jnp.exp(dot(x, section(2), 1, 1) + bias)))
-
-    tiles(n_tiles, project, {
-        0: [g.plane for g in gather_o],
-        2: [g.turn for g in gather_b],
-    })
+
+    def project_forget(i):
+        rows = rows_of(i, TM)
+        pre = dot(tok[rows, :], section(2), 1, 1) + bias
+        put(om, rows, 0, 1.0 / (1.0 + jnp.exp(pre)))
+
+    tiles(n_tiles, project, {1: [g.plane for g in gather_b]})
+    for g in gather_k:
+        g.ready()
+    tiles(n_tiles, project_forget, {1: [g.plane for g in gather_o]})
 
     def strided(t):
         return span(t * SEGS, SEGS)
@@ -581,15 +638,14 @@
     to_later, from_earlier = chain(carx, car_send, car_recv, True)
     to_later()
     for g in gather_b:
-        g.cross()
+        g.turn()
     for g in gather_o:
         g.turn()
     gather_f[0].plane()
-    for copy in load_cot:
-        copy.wait()
-    tiles(n_tiles, order_seed)
+    for g in gather_b:
+        g.cross()
     from_earlier()
-    gather_f[1].along()
+    gather_f[2].along()
     cr, ci = zrow, zrow
     for k in range(n_chan - 1):
         ar, ai = carx[k, 2:3, :], carx[k, 3:4, :]
@@ -637,8 +693,8 @@
         inv = lax.rsqrt(head_mean(yr * yr + yi * yi) + 1e-5)
         yr, yi = yr * inv, yi * inv
         rstd[rows, :] = inv
-        xh[rows, :half] = yr
-        xh[rows, half:] = yi
+        xh[rows, :half] = yr.astype(BF)
+        xh[rows, half:] = yi.astype(BF)
         lr, li = (yr * gain_r).astype(BF), (yi * gain_i).astype(BF)
         mix[rows, :half] = lr
         mix[rows, half:] = li
@@ -652,18 +708,17 @@
         dff[rows, :] = jnp.zeros((TM, width), F32)
 
     tiles(n_tiles, mixer_out, {
-        0: [gather_f[0].turn],
-        1: [gather_f[2].plane],
-        3: [gather_f[0].cross],
+        1: [gather_f[0].turn],
+        2: [gather_f[1].plane],
     })
 
     for j in range(n_chan):
-        cc = lax.rem(c + j, n_chan)
+        cc = lax.rem(c + ORDER[j], n_chan)
 
         def feed(i, cc=cc):
-            rows = rows_of(i, TM)
+            rows = rows_of(i, 2 * TM)
             gate_up = dot(fin[rows, :], w[cc, WG0:WD0, :], 1, 1)
-            d_hid = dot(sd[rows, :], w[cc, WD0:PIECE, :], 1, 1)
+            d_hid = dot(jnp.concatenate([sd[2 * i], sd[2 * i + 1]], axis=0), w[cc, WD0:PIECE, :], 1, 1)
             gate, up = gate_up[:, :hw], gate_up[:, hw:]
             sig = sigmoid(gate)
             act = gate * sig
@@ -677,11 +732,8 @@
             dff[rows, :] += dot(dgu[rows, :], w[cc, WG0:WD0, :], 1, 0)
 
         if j == 0:
-            tiles(n_tiles, feed, {
-                0: [gather_f[2].turn],
-                1: [gather_f[1].plane],
-                3: [gather_f[2].cross],
-            })
+            tiles(n_tiles // 2, feed, {1: [gather_f[0].cross]})
+            gather_f[1].turn()
             for g in gather_f:
                 g.along_free()
             gather_f[0].ready()
@@ -690,41 +742,56 @@
             older = [reduce_f[j - 2]] if j > 1 else []
             if j > 1:
                 gather_f[j - 1].ready()
-            tiles(n_tiles, feed, {
-                1: [r.turn for r in older],
-                2: [before.to_plane],
-                **({0: [gather_f[1].turn], 3: [gather_f[1].cross]} if j == 1 else {}),
+            tiles(n_tiles // 2, feed, {
+                1: ([gather_f[1].cross] if j == 1 else [])
+                + [r.pair_along for r in older] + [before.to_plane],
             })
+            if j == 2:
+                gather_f[2].cross()
             gather_f[j - 1].free()
         for k in range(2):
             w[cc, WG0 + hw * k : WG0 + hw * (k + 1), :] = dot(
                 dgu[:n_rows, hw * k : hw * (k + 1)], fin[...], 0, 0
             ).astype(BF)
-        w[cc, WD0:PIECE, :] = dot(hid[...], sd[...], 0, 0).astype(BF)
-        if j > 1:
-            older[0].along()
+        seeds = jnp.concatenate([sd[k] for k in range(n_tiles)], axis=0)
+        if j == 1:
+            gather_f[2].turn()
+        w[cc, WD0:PIECE, :] = dot(hid[...], seeds, 0, 0).astype(BF)
         reduce_f[j].to_core()
-
-    def mixer_back(i):
+        if j == 0:
+            gather_f[2].plane()
+
+    def norm_back(i):
         rows = rows_of(i, TM)
-        done = dot(swap[...], get(out, rows, 0, 2 * lt).astype(BF), 1, 0).astype(BF)
-        for k, at in enumerate(blocks(i)):
-            fin[at, :] = done[SEGS * k : SEGS * (k + 1), :]
+        fin[rows, :] = get(out, rows, 0, 2 * lt).astype(BF)
         r = res[rows, :]
         rinv = lax.rsqrt(jnp.mean(r * r, axis=1, keepdims=True) + 1e-6)
         rhat = r * rinv
         d = dff[rows, :]
         sgrad[2] += fold_rows(d * rhat)
         t = d * rms_gain
-        dres = sd[rows, :].astype(F32) + rinv * (
+        dres = sd[i].astype(F32) + rinv * (
             t - rhat * jnp.mean(t * rhat, axis=1, keepdims=True)
         )
         dff[rows, :] = dres
-        low = dres.astype(BF)
-        dm[i * TM // per, span(lax.rem(i * TM, per), TM), :] = low
+        dm[i, :TM, :] = dres.astype(BF)
+
+    tiles(n_tiles, norm_back)
+    reduce_f[-2].pair()
+    d_mixed = jnp.concatenate([dm[k, :TM, :] for k in range(n_tiles)], axis=0)
+    for k in range(2):
+        grad = dot(mix[:, k * half : (k + 1) * half], d_mixed, 0, 0).astype(BF)
+        for cc in range(n_chan):
+            sd[cc, 96 * k : 96 * k + 96, :] = grad[96 * cc : 96 * cc + 96, :]
+    reduce_o.to_core()
+    reduce_f[-1].to_plane()
+
+    def mixer_back(i):
+        rows = rows_of(i, TM)
+        low = dm[i, :TM, :]
         dr = dot(low, out_rows(0), 1, 1)
         di = dot(low, out_rows(1), 1, 1)
-        xr, xi = xh[rows, :half], xh[rows, half:]
+        xr, xi = xh[rows, :half].astype(F32), xh[rows, half:].astype(F32)
         sgrad[1, :, :half] += fold_rows(dr * xr)
         sgrad[1, :, half:] += fold_rows(di * xi)
         dr, di = dr * gain_r, di * gain_i
@@ -746,18 +813,13 @@
                 dy * state * (sig + act * (1.0 - sig))
             ).astype(BF)
             put(out, rows, k * lt, dy * act)
-        acc = dff[rows, :]
-        for k in range(3, 5):
-            acc += dot(dp[rows, k * half : (k + 1) * half], section(k), 1, 0)
-        dff[rows, :] = acc
-
-    tiles(n_tiles, mixer_back, {
-        1: [reduce_f[-2].turn, reduce_f[-1].to_plane],
-    })
-    out_copy = pltpu.make_async_copy(fin, out_hbm, store_sem.at[0])
-    out_copy.start()
-
-    reduce_f[-1].turn()
+    tiles(n_tiles, mixer_back, {2: [reduce_o.to_plane]})
+
+    def collect_f():
+        reduce_f[0].collect([copy for r in reduce_f[1:-1] for copy in r.s3])
+
+    def own_f():
+        reduce_f[0].add(reduce_f[0].s2)
 
     def first_back(k, carry):
         qr, qi = carry
@@ -790,25 +852,20 @@
     carb[c, 2:4, :] = carx[c, 2:4, :]
     to_earlier, from_later = chain(carb, cab_send, cab_recv, False)
     to_earlier()
-    reduce_f[-2].along()
-
-    for g in gather_a + gather_b + gather_o:
+    reduce_f[-2].send_along()
+
+    for g in gather_v + gather_k + gather_b + gather_o:
         g.along_free()
         g.free()
-    d_mixed = jnp.concatenate([dm[k, :per, :] for k in range(n_chan)], axis=0)
-    for k in range(4):
-        left = mix[:, k * half : (k + 1) * half] if k < 2 else dp[:, (k + 1) * half : (k + 2) * half]
-        grad = dot(left, d_mixed if k < 2 else tok[...], 0, 0).astype(BF)
-        to = WO0 + 96 * k if k < 2 else SECTION[k + 1]
+    for k in range(2):
+        grad = dot(dp[:, (3 + k) * half : (4 + k) * half], tok[...], 0, 0).astype(BF)
         for cc in range(n_chan):
-            w[cc, to : to + 96, :] = grad[96 * cc : 96 * cc + 96, :]
-        if k == 1:
-            reduce_o.to_core()
-    reduce_o.to_plane()
+            at = WO0 + 96 * k
+            w[cc, at : at + 96, :] = grad[96 * cc : 96 * cc + 96, :]
     reduce_g.to_core()
+    reduce_f[-1].turn()
 
     from_later()
-    reduce_f[-1].along()
     cr, ci = zrow, zrow
     for k in range(n_chan - 1, 0, -1):
         ar, ai = carb[k, 2:3, :], -carb[k, 3:4, :]
@@ -853,15 +910,15 @@
             )
         )
 
-    reduce_g.to_plane()
-    tiles(n_tiles, project_back)
+    tiles(n_tiles, project_back, {3: [reduce_f[-1].along]})
+    reduce_o.turn()
     for k in range(3):
         grad = dot(dp[:, k * half : (k + 1) * half], tok[...], 0, 0).astype(BF)
         for cc in range(n_chan):
             dm[cc, 96 * k : 96 * k + 96, :] = grad[96 * cc : 96 * cc + 96, :]
         if k == 1:
             reduce_v.to_core()
-            reduce_o.turn()
+            reduce_g.to_plane()
     small = jnp.concatenate(
         [jnp.sum(sgrad[k], axis=0, keepdims=True) for k in range(3)]
         + [jnp.zeros((29, width), F32)],
@@ -870,10 +927,15 @@
     for cc in range(n_chan):
         dm[cc, PAD0:MA0, :] = small
     reduce_k.to_core()
+    def order_out(i):
+        done = dot(swap[...], fin[rows_of(i, TM), :], 1, 0).astype(BF)
+        for k, at in enumerate(blocks(i)):
+            mix[at, :] = done[SEGS * k : SEGS * (k + 1), :]
+
     def d_tokens(i):
         rows = rows_of(i, TM)
         acc = dff[rows, :]
-        for k in range(3):
+        for k in range(5):
             acc += dot(dp[rows, k * half : (k + 1) * half], section(k), 1, 0)
         high = acc.astype(BF)
         low = (acc - high.astype(F32)).astype(BF)
@@ -882,24 +944,32 @@
             res[at, :] = done[SEGS * k : SEGS * (k + 1), :]
 
     tiles(n_tiles, d_tokens, {
-        1: [reduce_v.to_plane, reduce_g.turn],
-        2: [reduce_o.along, reduce_k.to_plane],
+        0: [reduce_o.along],
+        1: [reduce_v.to_plane],
+        2: [reduce_k.to_plane],
+        3: [collect_f],
     })
     gtok_copy = pltpu.make_async_copy(res, gtok_hbm, store_sem.at[1])
     gtok_copy.start()
     reduce_v.turn()
+    reduce_g.turn()
     reduce_k.turn()
+    own_f()
     spread_f.total()
+    tiles(n_tiles, order_out)
+    out_copy = pltpu.make_async_copy(mix, out_hbm, store_sem.at[0])
+    out_copy.start()
+    reduce_v.along()
+    spread_o.total()
+    reduce_k.along()
     reduce_g.along()
-    reduce_v.along()
-    reduce_k.along()
-    spread_o.total()
     spread_f.turn()
-    spread_g.total()
     spread_v.total()
     spread_k.total()
     spread_f.cross()
-    for sp in (spread_o, spread_g, spread_v, spread_k):
+    spread_o.cross()
+    spread_g.total()
+    for sp in (spread_v, spread_k, spread_g):
         sp.cross()
     spread_f.done()
     g_copies = [pltpu.make_async_copy(dgu, g_hbm.at[WG0:PIECE, :], store_sem.at[2])]
@@ -931,18 +1001,29 @@
         rows = pl.ds(cuts[k], cuts[k + 1] - cuts[k])
         loads.append(pltpu.make_async_copy(g_hbm.at[rows, :], g.at[rows, :], load_sem.at[k]))
         loads[-1].start()
-    stage = [
-        pltpu.make_async_copy(gtok_hbm, t_gtok, load_sem.at[5]),
-        pltpu.make_async_copy(out_hbm, t_block, load_sem.at[6]),
-    ]
-    for copy in stage:
-        copy.start()
+    through = []
+    for src, mid, dst in ((gtok_hbm, t_gtok, gtok_ref), (out_hbm, t_block, out_ref)):
+        n = mid.shape[0] // 4
+        for k in range(4):
+            rows = pl.ds(n * k, n)
+            sem = load_sem.at[5 + len(through)]
+            through.append((
+                pltpu.make_async_copy(src.at[rows, :], mid.at[rows, :], sem),
+                mid.at[rows, :], dst.at[rows, :],
+            ))
+            through[-1][0].start()
     stores = []
 
     def store(src, dst):
         copy = pltpu.make_async_copy(src, dst, store_sem.at[len(stores)])
         copy.start()
         stores.append(copy)
+
+    def pass_on(count):
+        for _ in range(count):
+            copy, mid, dst = through.pop(0)
+            copy.wait()
+            store(mid, dst)
 
     def joined(first):
         return jnp.concatenate(
@@ -972,23 +1053,25 @@
             gn_ref[:, to : to + HEAD_CH] = rows8[1:2, at : at + HEAD_CH]
     rows8[8:16, :] = pltpu.roll(small[0:8, :], 2 * turn, 1)
     rms_ref[...] = rows8[10:11, : 2 * nch]
+    pass_on(1)
     loads[1].wait()
     t_g[...] = joined(MA0).astype(F32)
     store(t_g, wg_ref)
     t_out[...] = joined(WO0).astype(F32)
     store(t_out, wout_ref)
+    pass_on(2)
     loads[2].wait()
     t_gate[...] = g[WG0 : WG0 + hw, :].T.astype(F32)
     store(t_gate, gate_ref)
+    pass_on(2)
     loads[3].wait()
     t_up[...] = g[WG0 + hw : WD0, :].T.astype(F32)
     store(t_up, up_ref)
+    pass_on(2)
     loads[4].wait()
     t_down[...] = g[WD0:PIECE, :].astype(F32)
     store(t_down, down_ref)
-    for copy, src, dst in zip(stage, (t_gtok, t_block), (gtok_ref, out_ref), strict=True):
-        copy.wait()
-        store(src, dst)
+    pass_on(1)
     for copy in stores:
         copy.wait()
 
@@ -1013,8 +1096,8 @@
         + [
             pltpu.VMEM(block_out.shape, BF),
             pltpu.VMEM((16, width), F32),
-            pltpu.SemaphoreType.DMA((7,)),
-            pltpu.SemaphoreType.DMA((9,)),
+            pltpu.SemaphoreType.DMA((13,)),
+            pltpu.SemaphoreType.DMA((15,)),
         ],
         compiler_params=pltpu.CompilerParams(vmem_limit_bytes=60 * 2**20),
         name="place",
@@ -1047,8 +1130,9 @@
         out_specs=[any_spec] * 3,
         scratch_shapes=[
             pltpu.VMEM(w_shape, BF),
-            full16, full16, full32, pltpu.VMEM((half // 128, rows, 128), F32), full32, tiles32,
-            full32, half32, full32, full16, full16, tiles32, full32,
+            full16, pltpu.VMEM((rows // TM, TM, width), BF), full32,
+            pltpu.VMEM((half // 128, rows, 128), F32), full32, tiles32,
+            full16, half32, full32, full16, full16, tiles32, full32,
             pltpu.VMEM((rows, hw), BF), pltpu.VMEM((PIECE - WG0, 2 * hw), BF),
             pltpu.VMEM((n_chan, MA0, width), BF), pltpu.VMEM((rows, 5 * half), BF),
             pltpu.VMEM((half, half), BF),
@@ -1065,7 +1149,8 @@
             pltpu.VMEM((3, n_chan, WG0 - WO0, half), BF),
             pltpu.VMEM((3, n_chan, (WG0 - WO0) // 2, half), BF),
             pltpu.VMEM((3, n_chan, (WG0 - WO0) // 4, half), BF),
-            pltpu.VMEM((n_chan - 1, (PIECE - WG0) // 4, half), BF),
+            pltpu.VMEM((2, (PIECE - WG0) // 2, half), BF),
+            pltpu.VMEM(((PIECE - WG0) // 4, half), BF),
             pltpu.VMEM((4, n_chan - 1, (WG0 - WO0) // 4, half), BF),
             pltpu.VMEM((WG0, width), BF),
             pltpu.VMEM((n_extra, (PIECE + 64) // 4, half) if n_batch > 8 else (1, 16, 128), BF),
@@ -1074,12 +1159,12 @@
             pltpu.SemaphoreType.DMA((4,)),
         ]
         + [pltpu.SemaphoreType.DMA((n_chan,))] * 6
-        + [pltpu.SemaphoreType.DMA((4 * (n_chan - 1), 9))] * 2
-        + [pltpu.SemaphoreType.DMA((n_chan + 4, 10))] * 2
+        + [pltpu.SemaphoreType.DMA((5 * (n_chan - 1), 9))] * 2
+        + [pltpu.SemaphoreType.DMA((n_chan + 4, 11))] * 2
         + [pltpu.SemaphoreType.DMA((5, 6))] * 2
         + [pltpu.SemaphoreType.DMA((5, n_extra))] * 2,
         compiler_params=pltpu.CompilerParams(
-            collective_id=0, has_side_effects=True, vmem_limit_bytes=62 * 2**20
+            collective_id=0, has_side_effects=True, vmem_limit_bytes=63 * 2**20
         ),
         cost_estimate=pl.CostEstimate(
             flops=34 * 10**9, bytes_accessed=3 * 10**7, transcendentals=0

time: 145 us -> 140 us (0.966)
  Pallas kernels: 143 us -> 137 us
    pallas_call x1, Pallas kernels: 136 us -> 131 us  [main_call(): pl.pallas_call(functools.partial(main_kernel, n_batch, n_chan), out_shape...]
where the time goes in v4:
time: 140 us; the launch traced here: 139 us
  Pallas kernels  137 us (98%)
  between operations  1.49 us (1%)
    pallas_call x1, Pallas kernels, main_call(): pl.pallas_call(functools.partial(main_kernel, n_batch, n_chan), out_shape...  131 us
    pallas_call x1, Pallas kernels, post_call(): pl.pallas_call(post_kernel, out_shape=[jax.ShapeDtypeStruct(shape, F32) f...  6.48 us

profile of v4, /device:TPU:0, one launch (start us, length us, event | category | flops | bytes accessed | tf_op | source)
XLA Modules:
  0.0 138.9 jit_solution(2465500876146785500)
XLA Ops:
  1.3 131.0 %block.1 = (bf16[1856,768]{1,0:T(8,128)(2,1)}, f32[1024,768]{1,0:T(8,128)}, bf16[1024,768]{1,0:T(8,128)(2,1)}) custom-call(bf16[192,768]{1,0:T(8,128)(2,1)} %bitcast.16, bf16[96,768]{1,0:T(8,128)(2,1)} %bitcast.19, bf16[192,768]{1,0:T(8,128)(2,1)} %bitcast.17, bf16[192,768]{1,0:T(8,128)(2,1)} %wout_hbm.1, bf16[768,384]{1,0:T(8,128)(2,1)} %wgate_hbm.1, ...), custom_call_target="tpu_custom_call" | custom-call | flops 33999998976 | bytes 30000000 | tf_op jit(solution)/shard_map/block/pallas_call | solution.py:1122
  132.3 6.5 %place.1 = (f32[192,768]{1,0:T(8,128)}, f32[96,768]{1,0:T(8,128)}, f32[1,96]{1,0:T(1,128)}, f32[1,96]{1,0:T(1,128)}, f32[192,768]{1,0:T(8,128)}, /*index=5*/f32[...) custom-call(bf16[1856,768]{1,0:T(8,128)(2,1)} %get-tuple-element.29., ...), custom_call_target="tpu_custom_call" | custom-call | tf_op jit(solution)/shard_map/place/pallas_call | solution.py:1088

commit v5 on v4

--- a/solution.py
+++ b/solution.py
@@ -947,13 +947,13 @@
         0: [reduce_o.along],
         1: [reduce_v.to_plane],
         2: [reduce_k.to_plane],
-        3: [collect_f],
     })
     gtok_copy = pltpu.make_async_copy(res, gtok_hbm, store_sem.at[1])
     gtok_copy.start()
     reduce_v.turn()
+    collect_f()
+    reduce_k.turn()
     reduce_g.turn()
-    reduce_k.turn()
     own_f()
     spread_f.total()
     tiles(n_tiles, order_out)
@@ -971,13 +971,19 @@
     spread_g.total()
     for sp in (spread_v, spread_k, spread_g):
         sp.cross()
-    spread_f.done()
-    g_copies = [pltpu.make_async_copy(dgu, g_hbm.at[WG0:PIECE, :], store_sem.at[2])]
-    g_copies[0].start()
-    for sp in (spread_o, spread_g, spread_v, spread_k):
+    g_copies = []
+
+    def leave(sp, src, rows):
         sp.done()
-    g_copies.append(pltpu.make_async_copy(mixf, g_hbm.at[:WG0, :], store_sem.at[3]))
-    g_copies[1].start()
+        copy = pltpu.make_async_copy(src, g_hbm.at[rows, :], store_sem.at[2 + len(g_copies)])
+        copy.start()
+        g_copies.append(copy)
+
+    leave(spread_f, dgu, pl.ds(WG0, PIECE - WG0))
+    for sp, lo, hi in (
+        (spread_o, WO0, WG0), (spread_v, 0, 2 * nch), (spread_k, 2 * nch, MA0), (spread_g, MA0, WO0)
+    ):
+        leave(sp, mixf.at[lo:hi, :], pl.ds(lo, hi - lo))
     for r in reduce_f + [reduce_o, reduce_g, reduce_v, reduce_k]:
         r.free()
     for copy in [out_copy, gtok_copy] + g_copies:
@@ -1156,7 +1162,7 @@
             pltpu.VMEM((n_extra, (PIECE + 64) // 4, half) if n_batch > 8 else (1, 16, 128), BF),
             pltpu.VMEM((8, half), F32),
             pltpu.SemaphoreType.DMA((5 + n_chan + 6 * nch // HEAD_CH,)),
-            pltpu.SemaphoreType.DMA((4,)),
+            pltpu.SemaphoreType.DMA((7,)),
         ]
         + [pltpu.SemaphoreType.DMA((n_chan,))] * 6
         + [pltpu.SemaphoreType.DMA((5 * (n_chan - 1), 9))] * 2

time: 140 us -> 139 us (level)
  no operation moved by 1% of the time
where the time goes in v5:
time: 139 us
  Pallas kernels  137 us (99%)
  between operations  1.49 us (1%)
    pallas_call x1, Pallas kernels, main_call(): pl.pallas_call(functools.partial(main_kernel, n_batch, n_chan), out_shape...  131 us
    pallas_call x1, Pallas kernels, post_call(): pl.pallas_call(post_kernel, out_shape=[jax.ShapeDtypeStruct(shape, F32) f...  6.48 us

profile of v5, /device:TPU:0, one launch (start us, length us, event | category | flops | bytes accessed | tf_op | source)
XLA Modules:
  0.0 138.6 jit_solution(8928924577113680723)
XLA Ops:
  1.3 130.7 %block.1 = (bf16[1856,768]{1,0:T(8,128)(2,1)}, f32[1024,768]{1,0:T(8,128)}, bf16[1024,768]{1,0:T(8,128)(2,1)}) custom-call(bf16[192,768]{1,0:T(8,128)(2,1)} %bitcast.16, bf16[96,768]{1,0:T(8,128)(2,1)} %bitcast.19, bf16[192,768]{1,0:T(8,128)(2,1)} %bitcast.17, bf16[192,768]{1,0:T(8,128)(2,1)} %wout_hbm.1, bf16[768,384]{1,0:T(8,128)(2,1)} %wgate_hbm.1, ...), custom_call_target="tpu_custom_call" | custom-call | flops 33999998976 | bytes 30000000 | tf_op jit(solution)/shard_map/block/pallas_call | solution.py:1128
  132.0 6.5 %place.1 = (f32[192,768]{1,0:T(8,128)}, f32[96,768]{1,0:T(8,128)}, f32[1,96]{1,0:T(1,128)}, f32[1,96]{1,0:T(1,128)}, f32[192,768]{1,0:T(8,128)}, /*index=5*/f32[...) custom-call(bf16[1856,768]{1,0:T(8,128)(2,1)} %get-tuple-element.29., ...), custom_call_target="tpu_custom_call" | custom-call | tf_op jit(solution)/shard_map/place/pallas_call | solution.py:1094

commit v6 on v5

--- a/solution.py
+++ b/solution.py
@@ -956,12 +956,12 @@
     reduce_g.turn()
     own_f()
     spread_f.total()
+    reduce_v.along()
+    spread_o.total()
+    reduce_k.along()
     tiles(n_tiles, order_out)
     out_copy = pltpu.make_async_copy(mix, out_hbm, store_sem.at[0])
     out_copy.start()
-    reduce_v.along()
-    spread_o.total()
-    reduce_k.along()
     reduce_g.along()
     spread_f.turn()
     spread_v.total()

time: 139 us -> 139 us (level)
  no operation moved by 1% of the time
where the time goes in v6:
time: 139 us
  Pallas kernels  137 us (99%)
  between operations  1.49 us (1%)
    pallas_call x1, Pallas kernels, main_call(): pl.pallas_call(functools.partial(main_kernel, n_batch, n_chan), out_shape...  131 us
    pallas_call x1, Pallas kernels, post_call(): pl.pallas_call(post_kernel, out_shape=[jax.ShapeDtypeStruct(shape, F32) f...  6.48 us

profile of v6, /device:TPU:0, one launch (start us, length us, event | category | flops | bytes accessed | tf_op | source)
XLA Modules:
  0.0 138.6 jit_solution(15599110083264537590)
XLA Ops:
  1.3 130.7 %block.1 = (bf16[1856,768]{1,0:T(8,128)(2,1)}, f32[1024,768]{1,0:T(8,128)}, bf16[1024,768]{1,0:T(8,128)(2,1)}) custom-call(bf16[192,768]{1,0:T(8,128)(2,1)} %bitcast.16, bf16[96,768]{1,0:T(8,128)(2,1)} %bitcast.19, bf16[192,768]{1,0:T(8,128)(2,1)} %bitcast.17, bf16[192,768]{1,0:T(8,128)(2,1)} %wout_hbm.1, bf16[768,384]{1,0:T(8,128)(2,1)} %wgate_hbm.1, ...), custom_call_target="tpu_custom_call" | custom-call | flops 33999998976 | bytes 30000000 | tf_op jit(solution)/shard_map/block/pallas_call | solution.py:1128
  132.0 6.5 %place.1 = (f32[192,768]{1,0:T(8,128)}, f32[96,768]{1,0:T(8,128)}, f32[1,96]{1,0:T(1,128)}, f32[1,96]{1,0:T(1,128)}, f32[192,768]{1,0:T(8,128)}, /*index=5*/f32[...) custom-call(bf16[1856,768]{1,0:T(8,128)(2,1)} %get-tuple-element.29., ...), custom_call_target="tpu_custom_call" | custom-call | tf_op jit(solution)/shard_map/place/pallas_call | solution.py:1094
